TPU v7x, 768 devices: a whole 4x8x12 slice. The times are simulated.
768 devices in a mesh: row: 16 (over y_lo, x, core), col: 48 (over z, y_hi).
Axes of the slice: x: 4, y: 8 (y_hi: 4, y_lo: 2; y = y_hi * 2 + y_lo), z: 12, core: 2. Of those that a mesh axis runs over, the one named last changes fastest.
Arguments:
- values: bfloat16 [6144, 6144], P('row', 'col'), may hold values from -6 to 6
- occupancy: int32 [48, 48], P('row', 'col'), may hold values 0 or 1
Outputs:
- square_slab: bfloat16 [4096, 6144], P('row', 'col')
- sign_step: bfloat16 [4096, 6144], P('row', 'col')
All inputs are finite; a program needn't handle non-finite values. No bound on the sum of `occupancy` on one device may be relied on, other than what follows from the above.
Results may differ from a plain program's by a relative error of at most 0.0015.
Values may be sent and summed in bfloat16 or wider, within the bound.
No kernel may reach another device: no remote copies, remote signals or barrier semaphores. Data moves between devices by JAX's collectives and lax.ppermute only.
A program may use at most 32 MiB of HBM per device.

v0:
```python
import math

import jax
import jax.numpy as jnp
from jax import lax
from jax.sharding import PartitionSpec as P

BS = 128
SLAB = 256


def local(values, occupancy):
    block_mask = jnp.repeat(jnp.repeat(occupancy, BS, 0), BS, 1).astype(jnp.float32)
    masked = (values.astype(jnp.float32) * block_mask).astype(jnp.bfloat16)
    columns = lax.all_gather(masked, "row", axis=0, tiled=True)
    factor = 1.0 / math.sqrt(columns.shape[0])
    slab_part = masked[:SLAB]
    slab_mask = block_mask[:SLAB]
    gathered = lax.all_gather(slab_part, "col", axis=1, tiled=True)
    first_sum = jnp.dot(gathered, columns, preferred_element_type=jnp.float32)
    square_slab = (first_sum * factor * slab_mask).astype(jnp.bfloat16)
    square_whole = lax.all_gather(square_slab, "col", axis=1, tiled=True)
    second_sum = jnp.dot(square_whole, columns, preferred_element_type=jnp.float32)
    sign_step = (
        (1.5 * slab_part.astype(jnp.float32) - 0.5 * factor * second_sum) * slab_mask
    ).astype(jnp.bfloat16)
    return (square_slab, sign_step)


def solution(mesh):
    in_specs = (P("row", "col"), P("row", "col"))
    out_specs = (P("row", "col"), P("row", "col"))
    return jax.shard_map(local, mesh=mesh, in_specs=in_specs, out_specs=out_specs, check_vma=False)
```

profile of v0, /device:TPU:6, one launch (start us, length us, event | category | flops | bytes accessed | tf_op | source)
XLA Modules:
  0.0 316.1 jit_solution(2092011626200635379)
XLA Ops:
  7.2 0.0 all-gather.6.cloned.1.call-start
  7.2 0.7 fusion.4
  7.9 0.1 broadcast_bitcast_fusion
  7.9 1.6 multiply_convert_fusion
  9.6 0.0 copy-start.1
  9.6 0.0 all-gather.6.cloned.1.call-update
  9.6 0.0 all-gather.4.cloned.1.call-start
  9.7 1.5 slice.18
  11.1 0.0 all-gather.4.cloned.1.call-update
  11.2 0.0 all-gather.8.cloned.1.call-start
  11.2 0.1 bitcast_multiply_fusion
  11.3 46.3 %all-gather.6.cloned.1.call-done = bf16[6144,128]{1,0:T(8,128)(2,1)} async-done(((bf16[384,128]{1,0:T(8,128)(2,1)}), bf16[6144,128]{1,0:T(8,128)(2,1)}) %all-gather.6.cloned.1.call-update) | async-done | bytes 1572880 | tf_op jit(solution)/shard_map/all_gather | solution.py:15
  57.6 0.0 copy-start
  57.6 127.4 %all-gather.4.cloned.1.call-done = bf16[256,6144]{1,0:T(8,128)(2,1)} async-done(((bf16[256,128]{1,0:T(8,128)(2,1)}), bf16[256,6144]{1,0:T(8,128)(2,1)}) %all-gather.4.cloned.1.call-update) | async-done | bytes 3145744 | tf_op jit(solution)/shard_map/all_gather | solution.py:19
  185.0 4.0 %fusion.2 = bf16[256,128]{1,0:T(8,128)(2,1)} fusion(bf16[256,6144]{1,0:T(8,128)(2,1)} %all-gather.4.cloned.1.call-done, bf16[6144,128]{1,0:T(8,128)(2,1)} %all-gather.6.cloned.1.call-done, f32[256]{0:T(256)S(1)} %bitcast_multiply_fusion), kind=kOutput, calls=%fused_computation.4 | convolution fusion | flops 402718720 | bytes 4785152 | tf_op jit(solution)/shard_map/dot_general | solution.py:20
  188.9 0.0 all-gather.8.cloned.1.call-update
  189.0 0.1 broadcast_bitcast_fusion.1
  189.0 117.0 %all-gather.8.cloned.1.call-done = bf16[256,6144]{1,0:T(8,128)(2,1)} async-done(((bf16[256,128]{1,0:T(8,128)(2,1)}), bf16[256,6144]{1,0:T(8,128)(2,1)}) %all-gather.8.cloned.1.call-update) | async-done | bytes 3145744 | tf_op jit(solution)/shard_map/all_gather | solution.py:22
  306.1 0.0 copy-done.1
  306.1 0.0 copy-done
  306.1 3.5 %fusion.3 = bf16[256,128]{1,0:T(8,128)(2,1)} fusion(bf16[256,6144]{1,0:T(8,128)(2,1)} %all-gather.8.cloned.1.call-done, bf16[6144,128]{1,0:T(8,128)(2,1)S(1)} %copy-done, f32[256]{0:T(256)S(1)} %broadcast_bitcast_fusion.1, bf16[384,128]{1,0:T(8,128)(2,1)S(1)} %copy-done.1), kind=kOutput, calls=%fused_computation.5 | convolution fusion | flops 402849792 | bytes 4850688 | tf_op jit(solution)/shard_map/dot_general | solution.py:23
  (1 shorter events, 0.0 us)
Async XLA Ops:
  7.2 50.4 %all-gather.6.cloned.1.call-start = ((), (), s32[]{:S(2)}) async-start(), calls=%async_computation.1 | async-start | bytes 1671168 | tf_op jit(solution)/shard_map/all_gather | solution.py:15
  9.6 296.5 %copy-start.1 = (bf16[384,128]{1,0:T(8,128)(2,1)S(1)}, bf16[384,128]{1,0:T(8,128)(2,1)}, u32[]{:S(2)}) copy-start(bf16[384,128]{1,0:T(8,128)(2,1)} %multiply_convert_fusion) | copy-start | bytes 294916
  9.6 175.4 %all-gather.4.cloned.1.call-start = ((), (), s32[]{:S(2)}) async-start(), calls=%async_computation | async-start | bytes 3211264 | tf_op jit(solution)/shard_map/all_gather | solution.py:19
  11.2 294.9 %all-gather.8.cloned.1.call-start = ((), (), s32[]{:S(2)}) async-start(), calls=%async_computation.2 | async-start | bytes 3211264 | tf_op jit(solution)/shard_map/all_gather | solution.py:22
  57.6 248.5 %copy-start = (bf16[6144,128]{1,0:T(8,128)(2,1)S(1)}, bf16[6144,128]{1,0:T(8,128)(2,1)}, u32[]{:S(2)}) copy-start(bf16[6144,128]{1,0:T(8,128)(2,1)} %all-gather.6.cloned.1.call-done) | copy-start | bytes 4718596
Sparse Core Ops, SparseCore 0:
  10.4 47.0 all-gather.5
  61.7 123.2 all-gather.3
  189.1 116.9 all-gather.7
where the time goes:
time: 317 us; the launch traced here: 316 us
  waiting for transfers between devices  291 us (92%)
  between operations  13.8 us (4%)
  matrix products  7.45 us (2%)
    all_gather x1, waiting for transfers between devices, local(): gathered = lax.all_gather(slab_part, 'col', axis=1, tiled=True)  127 us
    all_gather x1, waiting for transfers between devices, local(): square_whole = lax.all_gather(square_slab, 'col', axis=1, tiled=True)  117 us
    all_gather x1, waiting for transfers between devices, local(): columns = lax.all_gather(masked, 'row', axis=0, tiled=True)  46.3 us
  transfers between devices with their start and end apart: 3, of which 3 were waited for; matrix products, arithmetic and copies ran while one was open for 1% of the time, Pallas kernels for 0%

commit v1 on v0

v1 whole, which is shorter than its diff:
```python
import math

import jax
import jax.numpy as jnp
from jax import lax
from jax.experimental import pallas as pl
from jax.experimental.pallas import tpu as pltpu
from jax.sharding import Mesh
from jax.sharding import PartitionSpec as P

BS = 128
SLAB = 256
ORDER = 6144
FACTOR = 1.0 / math.sqrt(ORDER)
N_YL, N_X, N_CORE, N_Z, N_YH = 2, 4, 2, 12, 4
LIMIT = 24 * 1024 * 1024


def vmem(n):
    return [pl.BlockSpec(memory_space=pltpu.VMEM)] * n


def smem(n):
    return [pl.BlockSpec(memory_space=pltpu.SMEM)] * n


def position():
    yl, x, core = lax.axis_index("yl"), lax.axis_index("x"), lax.axis_index("core")
    return jnp.stack([(yl * N_X + x) * N_CORE + core, core, lax.axis_index("yh")])


def prepare(pos_ref, occ_ref, values_ref, slab_ref, send_ref):
    for t in range(2):
        rows = pl.ds(t * BS, BS)
        slab_ref[rows, :] = values_ref[rows, :] * occ_ref[t].astype(jnp.float32).astype(jnp.bfloat16)
    first = 3 * pos_ref[0]
    for q in range(N_YH):
        t = lax.rem(q + 4 * 48 - first, 4)
        held = jnp.minimum(t, 2)
        keep = jnp.where(t < 3, occ_ref[held], 0).astype(jnp.float32).astype(jnp.bfloat16)
        block = values_ref[pl.ds(pl.multiple_of(held * BS, BS), BS), :] * keep
        for j in range(N_YL * N_X):
            send_ref[j * N_YH + q] = block


def assemble(s_ref, sk_ref):
    for z in range(N_Z):
        sk_ref[:, z * BS:(z + 1) * BS] = s_ref[z]


def first_product(pos_ref, s_ref, mine_ref, other_ref, out_ref, mk_ref, sk_ref):
    assemble(s_ref, sk_ref)
    my_core, yh = pos_ref[1], pos_ref[2]
    for z in range(N_Z):
        r = lax.div(4 * z + yh, 3)
        slot = lax.div(r, 2) * N_YH
        here = lax.rem(r, 2) == my_core

        @pl.when(here)
        def _():
            for q in range(N_YH):
                mk_ref[z * BS:(z + 1) * BS, q * BS:(q + 1) * BS] = mine_ref[slot + q]

        @pl.when(jnp.logical_not(here))
        def _():
            for q in range(N_YH):
                mk_ref[z * BS:(z + 1) * BS, q * BS:(q + 1) * BS] = other_ref[slot + q]

    total = jnp.dot(sk_ref[...], mk_ref[...], preferred_element_type=jnp.float32)
    for q in range(N_YH):
        out_ref[q] = total[:, q * BS:(q + 1) * BS]


def second_product(s_ref, mk_ref, out_ref, sk_ref):
    assemble(s_ref, sk_ref)
    total = jnp.dot(sk_ref[...], mk_ref[...], preferred_element_type=jnp.float32)
    for q in range(N_YH):
        out_ref[q] = total[:, q * BS:(q + 1) * BS]


def finish_square(occ_ref, parts_ref, out_ref):
    for t in range(2):
        rows = pl.ds(t * BS, BS)
        total = (parts_ref[0, rows, :] + parts_ref[1, rows, :]) + (parts_ref[2, rows, :] + parts_ref[3, rows, :])
        out_ref[rows, :] = (total * FACTOR * occ_ref[t].astype(jnp.float32)).astype(jnp.bfloat16)


def finish_sign(occ_ref, slab_ref, parts_ref, out_ref):
    for t in range(2):
        rows = pl.ds(t * BS, BS)
        total = (parts_ref[0, rows, :] + parts_ref[1, rows, :]) + (parts_ref[2, rows, :] + parts_ref[3, rows, :])
        step = 1.5 * slab_ref[rows, :].astype(jnp.float32) - 0.5 * FACTOR * total
        out_ref[rows, :] = (step * occ_ref[t].astype(jnp.float32)).astype(jnp.bfloat16)


def shape(*dims, dtype=jnp.bfloat16):
    return jax.ShapeDtypeStruct(dims, dtype)


def kernel(body, n_smem, n_vmem, out_shape, scratch=(), flops=0, moved=1 << 20):
    return pl.pallas_call(
        body,
        out_shape=out_shape,
        in_specs=smem(n_smem) + vmem(n_vmem),
        out_specs=jax.tree.map(lambda _: pl.BlockSpec(memory_space=pltpu.VMEM), out_shape),
        scratch_shapes=list(scratch),
        compiler_params=pltpu.CompilerParams(vmem_limit_bytes=LIMIT),
        cost_estimate=pl.CostEstimate(flops=flops, bytes_accessed=moved, transcendentals=0),
    )


def local(values, occupancy):
    occ = occupancy.reshape(3)
    pos = position()
    group = N_YL * N_X * N_YH
    slab, send = kernel(prepare, 2, 1, (shape(SLAB, BS), shape(group, BS, BS)))(pos, occ, values)
    mine = lax.all_to_all(send, ("yl", "x", "yh"), 0, 0, tiled=True)
    other = lax.ppermute(mine, "core", [(0, 1), (1, 0)])
    gathered = lax.all_gather(slab, "z", axis=0, tiled=False)
    cost = dict(flops=2 * SLAB * 12 * BS * 4 * BS, moved=4 << 20)
    sk = pltpu.VMEM((SLAB, N_Z * BS), jnp.bfloat16)
    parts_shape = shape(N_YH, SLAB, BS, dtype=jnp.float32)
    parts, mk = kernel(
        first_product, 1, 3, (parts_shape, shape(N_Z * BS, N_YH * BS)), (sk,), **cost
    )(pos, gathered, mine, other)
    parts = lax.all_to_all(parts, "yh", 0, 0, tiled=True)
    square_slab = kernel(finish_square, 1, 1, shape(SLAB, BS))(occ, parts)
    gathered = lax.all_gather(square_slab, "z", axis=0, tiled=False)
    parts = kernel(second_product, 0, 2, parts_shape, (sk,), **cost)(gathered, mk)
    parts = lax.all_to_all(parts, "yh", 0, 0, tiled=True)
    sign_step = kernel(finish_sign, 1, 2, shape(SLAB, BS))(occ, slab, parts)
    return (square_slab, sign_step)


def solution(mesh):
    fine = Mesh(
        mesh.devices.reshape(N_YL, N_X, N_CORE, N_Z, N_YH), ("yl", "x", "core", "z", "yh")
    )
    spec = P(("yl", "x", "core"), ("z", "yh"))
    return jax.shard_map(local, mesh=fine, in_specs=(spec, spec), out_specs=(spec, spec), check_vma=False)
```

time: 317 us -> 141 us (0.44)
  waiting for transfers between devices: 291 us -> 0.01 us
  blocking collectives: 0 us -> 130 us
  between operations: 13.8 us -> 0.68 us
  matrix products: 7.45 us -> 0 us
  Pallas kernels: 0 us -> 5.31 us
    all_gather x3 -> x0, waiting for transfers between devices: 291 us -> none  [the longest x1 127 us: local(): gathered = lax.all_gather(slab_part, 'col', axis=1, tiled=True)]
    all_to_all x0 -> x3, blocking collectives: none -> 68.2 us  [the longest x1 36.1 us: local(): mine = lax.all_to_all(send, ('yl', 'x', 'yh'), 0, 0, tiled=True)]
    all_gather x0 -> x2, blocking collectives: none -> 61.9 us  [the longest x1 37.4 us: local(): gathered = lax.all_gather(slab, 'z', axis=0, tiled=False)]
    dot_general x2 -> x0, matrix products: 7.45 us -> none  [the longest x1 3.95 us: local(): first_sum = jnp.dot(gathered, columns, preferred_element_type=jnp.float32)]
    pallas_call x0 -> x5, Pallas kernels: none -> 5.31 us  [the longest x1 1.68 us: local(): kernel(first_product, 1, 3, (parts_shape, shape(N_Z * BS, N_YH * BS)), (s...]
  transfers between devices with their start and end apart: 3 -> 1, of which waited for: 3 -> 0; matrix products, arithmetic and copies ran while one was open for 1% -> 0% of each run, Pallas kernels for 0% -> 0%
where the time goes in v1:
time: 141 us; the launch traced here: 140 us
  blocking collectives  130 us (92%)
  Pallas kernels  5.31 us (4%)
  starting transfers between devices  1.91 us (1%)
  local copies, waits for them, and re-layouts  1.55 us (1%)
    all_gather x1, blocking collectives, local(): gathered = lax.all_gather(slab, 'z', axis=0, tiled=False)  37.4 us
    all_to_all x1, blocking collectives, local(): mine = lax.all_to_all(send, ('yl', 'x', 'yh'), 0, 0, tiled=True)  36.1 us
    all_to_all x2, blocking collectives, local(): parts = lax.all_to_all(parts, 'yh', 0, 0, tiled=True)  32.1 us
    all_gather x1, blocking collectives, local(): gathered = lax.all_gather(square_slab, 'z', axis=0, tiled=False)  24.5 us
  transfers between devices with their start and end apart: 1, of which 0 were waited for; matrix products, arithmetic and copies ran while one was open for 0% of the time, Pallas kernels for 0%

profile of v1, /device:TPU:6, one launch (start us, length us, event | category | flops | bytes accessed | tf_op | source)
XLA Modules:
  0.0 139.6 jit_solution(18125390656724124019)
XLA Ops:
  0.6 0.1 pad_add_fusion.pos_ref
  0.7 0.0 copy-start
  0.7 0.9 copy-done
  1.6 0.0 copy-start.1
  1.6 0.7 copy-done.1
  2.3 0.6 shard_map.41
  2.9 36.1 %all_to_all.15.mine_ref = bf16[32,128,128]{2,1,0:T(8,128)(2,1)S(1)} all-to-all(bf16[32,128,128]{2,1,0:T(8,128)(2,1)S(1)} %get-tuple-element.7), channel_id=1, replica_groups=mesh['yl'=2,'x'=4,'core'=2,'z'=12,'yh'=4] {'yl','x','yh'}, dimensions={0} | all-to-all | bytes 2097152 | tf_op jit(solution)/shard_map/all_to_all | solution.py:117
  39.0 1.9 %collective-permute-start = (bf16[32,128,128]{2,1,0:T(8,128)(2,1)S(1)}, bf16[32,128,128]{2,1,0:T(8,128)(2,1)S(1)}, u32[]{:S(2)}, u32[]{:S(2)}) collective-permute-start(bf16[32,128,128]{2,1,0:T(8,128)(2,1)S(1)} %all_to_all.15.mine_ref), channel_id=1, source_target_pairs={{0,48},{48,0},{1,49},{49,1},{2,50},{50,2},{3,51},{51,3},{4,52},{52... | collective-permute-start | bytes 3145736 | tf_op jit(solution)/shard_map/ppermute | solution.py:118
  40.9 37.4 %all-gather = bf16[3072,128]{1,0:T(8,128)(2,1)S(1)} all-gather(bf16[256,128]{1,0:T(8,128)(2,1)S(1)} %get-tuple-element.6.slab_ref), channel_id=2, replica_groups=mesh['yl'=2,'x'=4,'core'=2,'z'=12,'yh'=4] {'z'}, dimensions={0}, use_global_device_ids=true | all-gather | bytes 851968 | tf_op jit(solution)/shard_map/all_gather | solution.py:119
  78.2 0.0 collective-permute-done.other_ref
  78.2 1.7 %shard_map.42 = (f32[4,256,128]{2,1,0:T(8,128)S(1)}, bf16[1536,512]{1,0:T(8,128)(2,1)S(1)}) custom-call(s32[3]{0:T(128)S(1)} %pad_add_fusion.pos_ref, bf16[12,256,128]{2,1,0:T(8,128)(2,1)S(1)} %bitcast.6, bf16[32,128,128]{2,1,0:T(8,128)(2,1)S(1)} %all_to_all.15.mine_ref, bf16[32,128,128]{2,1,0:T(8,128)(2,1)S(1)} %collective-permute-done.other_ref), custom_call_target="tpu_custom_call" | custom-call | flops 402653184 | bytes 4194304 | tf_op jit(solution)/shard_map/pallas_call | solution.py:123
  79.9 16.7 %all_to_all.16.parts_ref = f32[4,256,128]{2,1,0:T(8,128)S(1)} all-to-all(f32[4,256,128]{2,1,0:T(8,128)S(1)} %get-tuple-element.8), channel_id=1, replica_groups=mesh['yl'=2,'x'=4,'core'=2,'z'=12,'yh'=4] {'yh'}, dimensions={0} | all-to-all | bytes 1048576 | tf_op jit(solution)/shard_map/all_to_all | solution.py:126
  96.6 1.2 shard_map.43
  97.8 24.5 %all-gather.1 = bf16[3072,128]{1,0:T(8,128)(2,1)S(1)} all-gather(bf16[256,128]{1,0:T(8,128)(2,1)} %shard_map.43), channel_id=3, replica_groups=mesh['yl'=2,'x'=4,'core'=2,'z'=12,'yh'=4] {'z'}, dimensions={0}, use_global_device_ids=true | all-gather | bytes 851968 | tf_op jit(solution)/shard_map/all_gather | solution.py:128
  122.3 0.6 shard_map.44
  122.9 15.4 %all_to_all.17.parts_ref = f32[4,256,128]{2,1,0:T(8,128)S(1)} all-to-all(f32[4,256,128]{2,1,0:T(8,128)S(1)} %shard_map.44), channel_id=1, replica_groups=mesh['yl'=2,'x'=4,'core'=2,'z'=12,'yh'=4] {'yh'}, dimensions={0} | all-to-all | bytes 1048576 | tf_op jit(solution)/shard_map/all_to_all | solution.py:130
  138.4 1.2 shard_map.45
Async XLA Ops:
  0.7 0.9 copy-start
  1.6 0.7 copy-start.1
  39.0 39.3 %collective-permute-start = (bf16[32,128,128]{2,1,0:T(8,128)(2,1)S(1)}, bf16[32,128,128]{2,1,0:T(8,128)(2,1)S(1)}, u32[]{:S(2)}, u32[]{:S(2)}) collective-permute-start(bf16[32,128,128]{2,1,0:T(8,128)(2,1)S(1)} %all_to_all.15.mine_ref), channel_id=1, source_target_pairs={{0,48},{48,0},{1,49},{49,1},{2,50},{50,2},{3,51},{51,3},{4,52},{52... | collective-permute-start | bytes 3145736 | tf_op jit(solution)/shard_map/ppermute | solution.py:118

commit v2 on v1

--- a/solution.py
+++ b/solution.py
@@ -115,8 +115,9 @@
     group = N_YL * N_X * N_YH
     slab, send = kernel(prepare, 2, 1, (shape(SLAB, BS), shape(group, BS, BS)))(pos, occ, values)
     mine = lax.all_to_all(send, ("yl", "x", "yh"), 0, 0, tiled=True)
+    gathered = lax.all_gather(slab, "z", axis=0, tiled=False)
+    mine, gathered = lax.optimization_barrier((mine, gathered))
     other = lax.ppermute(mine, "core", [(0, 1), (1, 0)])
-    gathered = lax.all_gather(slab, "z", axis=0, tiled=False)
     cost = dict(flops=2 * SLAB * 12 * BS * 4 * BS, moved=4 << 20)
     sk = pltpu.VMEM((SLAB, N_Z * BS), jnp.bfloat16)
     parts_shape = shape(N_YH, SLAB, BS, dtype=jnp.float32)

time: 141 us -> 126 us (0.89)
  blocking collectives: 130 us -> 97.7 us
  starting transfers between devices: 1.91 us -> 15.2 us
  waiting for transfers between devices: 0.01 us -> 2.63 us
    all_to_all x1 -> x0, blocking collectives: 36.1 us -> none  [local(): mine = lax.all_to_all(send, ('yl', 'x', 'yh'), 0, 0, tiled=True)]
    all_to_all x0 -> x1, starting transfers between devices: none -> 13.1 us  [local(): mine = lax.all_to_all(send, ('yl', 'x', 'yh'), 0, 0, tiled=True)]
    all_to_all x2, blocking collectives: 32.1 us -> 38.7 us  [local(): parts = lax.all_to_all(parts, 'yh', 0, 0, tiled=True)]
    all_gather x1, blocking collectives: 37.4 us -> 34.4 us  [local(): gathered = lax.all_gather(slab, 'z', axis=0, tiled=False)]
    ppermute x1, waiting for transfers between devices: 0.01 us -> 2.63 us  [local(): other = lax.ppermute(mine, 'core', [(0, 1), (1, 0)])]
  transfers between devices with their start and end apart: 1 -> 2, of which waited for: 0 -> 1; matrix products, arithmetic and copies ran while one was open for 0% -> 0% of each run, Pallas kernels for 0% -> 0%
where the time goes in v2:
time: 126 us; the launch traced here: 124 us
  blocking collectives  97.7 us (78%)
  starting transfers between devices  15.2 us (12%)
  Pallas kernels  6.29 us (5%)
  waiting for transfers between devices  2.63 us (2%)
  local copies, waits for them, and re-layouts  1.55 us (1%)
    all_to_all x2, blocking collectives, local(): parts = lax.all_to_all(parts, 'yh', 0, 0, tiled=True)  38.7 us
    all_gather x1, blocking collectives, local(): gathered = lax.all_gather(slab, 'z', axis=0, tiled=False)  34.4 us
    all_gather x1, blocking collectives, local(): gathered = lax.all_gather(square_slab, 'z', axis=0, tiled=False)  24.6 us
    all_to_all x1, starting transfers between devices, local(): mine = lax.all_to_all(send, ('yl', 'x', 'yh'), 0, 0, tiled=True)  13.1 us
    ppermute x1, waiting for transfers between devices, local(): other = lax.ppermute(mine, 'core', [(0, 1), (1, 0)])  2.63 us
  transfers between devices with their start and end apart: 2, of which 1 were waited for; matrix products, arithmetic and copies ran while one was open for 0% of the time, Pallas kernels for 0%

profile of v2, /device:TPU:6, one launch (start us, length us, event | category | flops | bytes accessed | tf_op | source)
XLA Modules:
  0.0 124.1 jit_solution(3856388192675113614)
XLA Ops:
  0.6 0.1 pad_add_fusion.pos_ref
  0.7 0.0 copy-start
  0.7 0.9 copy-done
  1.6 0.0 copy-start.1
  1.6 0.7 copy-done.1
  2.3 1.6 %shard_map.41 = (bf16[256,128]{1,0:T(8,128)(2,1)S(1)}, bf16[32,128,128]{2,1,0:T(8,128)(2,1)}) custom-call(s32[3]{0:T(128)S(1)} %pad_add_fusion.pos_ref, s32[3]{0:T(128)S(1)} %bitcast.8, bf16[384,128]{1,0:T(8,128)(2,1)S(1)} %copy-done), custom_call_target="tpu_custom_call" | custom-call | bytes 1048576 | tf_op jit(solution)/shard_map/pallas_call | solution.py:116
  3.9 13.1 %all-to-all-start = ((bf16[32,128,128]{2,1,0:T(8,128)(2,1)}), bf16[32,128,128]{2,1,0:T(8,128)(2,1)S(1)}, u32[]{:S(2)}, u32[]{:S(2)}) async-start(bf16[32,128,128]{2,1,0:T(8,128)(2,1)} %get-tuple-element.8), calls=%async_computation | async-start | bytes 2097152 | tf_op jit(solution)/shard_map/all_to_all | solution.py:117
  17.0 34.4 %all-gather = bf16[3072,128]{1,0:T(8,128)(2,1)S(1)} all-gather(bf16[256,128]{1,0:T(8,128)(2,1)S(1)} %get-tuple-element.9.slab_ref), channel_id=2, replica_groups=mesh['yl'=2,'x'=4,'core'=2,'z'=12,'yh'=4] {'z'}, dimensions={0}, use_global_device_ids=true | all-gather | bytes 851968 | tf_op jit(solution)/shard_map/all_gather | solution.py:118
  51.4 0.0 all-to-all-done.mine_ref
  51.4 0.0 copy-start.2
  51.4 2.0 %collective-permute-start = (bf16[32,128,128]{2,1,0:T(8,128)(2,1)S(1)}, bf16[32,128,128]{2,1,0:T(8,128)(2,1)S(1)}, u32[]{:S(2)}, u32[]{:S(2)}) collective-permute-start(bf16[32,128,128]{2,1,0:T(8,128)(2,1)S(1)} %all-to-all-done.mine_ref), channel_id=1, source_target_pairs={{0,48},{48,0},{1,49},{49,1},{2,50},{50,2},{3,51},{51,3},{4,52},{52... | collective-permute-start | bytes 3145736 | tf_op jit(solution)/shard_map/ppermute | solution.py:120
  53.4 2.6 %collective-permute-done.other_ref = bf16[32,128,128]{2,1,0:T(8,128)(2,1)S(1)} collective-permute-done((bf16[32,128,128]{2,1,0:T(8,128)(2,1)S(1)}, bf16[32,128,128]{2,1,0:T(8,128)(2,1)S(1)}, u32[]{:S(2)}, u32[]{:S(2)}) %collective-permute-start) | collective-permute-done | bytes 1048608 | tf_op jit(solution)/shard_map/ppermute | solution.py:120
  56.1 1.7 %shard_map.42 = (f32[4,256,128]{2,1,0:T(8,128)S(1)}, bf16[1536,512]{1,0:T(8,128)(2,1)S(1)}) custom-call(s32[3]{0:T(128)S(1)} %pad_add_fusion.pos_ref, bf16[12,256,128]{2,1,0:T(8,128)(2,1)S(1)} %bitcast.6, bf16[32,128,128]{2,1,0:T(8,128)(2,1)S(1)} %all-to-all-done.mine_ref, bf16[32,128,128]{2,1,0:T(8,128)(2,1)S(1)} %collective-permute-done.other_ref), custom_call_target="tpu_custom_call" | custom-call | flops 402653184 | bytes 4194304 | tf_op jit(solution)/shard_map/pallas_call | solution.py:124
  57.8 23.0 %all_to_all.15.parts_ref = f32[4,256,128]{2,1,0:T(8,128)S(1)} all-to-all(f32[4,256,128]{2,1,0:T(8,128)S(1)} %get-tuple-element.12), channel_id=1, replica_groups=mesh['yl'=2,'x'=4,'core'=2,'z'=12,'yh'=4] {'yh'}, dimensions={0} | all-to-all | bytes 1048576 | tf_op jit(solution)/shard_map/all_to_all | solution.py:127
  80.8 0.0 copy-done.2
  80.8 1.2 shard_map.43
  82.0 24.6 %all-gather.1 = bf16[3072,128]{1,0:T(8,128)(2,1)S(1)} all-gather(bf16[256,128]{1,0:T(8,128)(2,1)} %shard_map.43), channel_id=3, replica_groups=mesh['yl'=2,'x'=4,'core'=2,'z'=12,'yh'=4] {'z'}, dimensions={0}, use_global_device_ids=true | all-gather | bytes 851968 | tf_op jit(solution)/shard_map/all_gather | solution.py:129
  106.6 0.6 shard_map.44
  107.2 15.7 %all_to_all.16.parts_ref = f32[4,256,128]{2,1,0:T(8,128)S(1)} all-to-all(f32[4,256,128]{2,1,0:T(8,128)S(1)} %shard_map.44), channel_id=1, replica_groups=mesh['yl'=2,'x'=4,'core'=2,'z'=12,'yh'=4] {'yh'}, dimensions={0} | all-to-all | bytes 1048576 | tf_op jit(solution)/shard_map/all_to_all | solution.py:131
  122.9 1.2 shard_map.45
Async XLA Ops:
  0.7 0.9 copy-start
  1.6 0.7 copy-start.1
  3.9 47.5 %all-to-all-start = ((bf16[32,128,128]{2,1,0:T(8,128)(2,1)}), bf16[32,128,128]{2,1,0:T(8,128)(2,1)S(1)}, u32[]{:S(2)}, u32[]{:S(2)}) async-start(bf16[32,128,128]{2,1,0:T(8,128)(2,1)} %get-tuple-element.8), calls=%async_computation | async-start | bytes 2097152 | tf_op jit(solution)/shard_map/all_to_all | solution.py:117
  51.4 29.4 %copy-start.2 = (s32[3,1]{0,1:T(1,128)S(1)}, s32[3,1]{0,1:T(1,128)}, u32[]{:S(2)}) copy-start(s32[3,1]{0,1:T(1,128)} %param.3) | copy-start | bytes 40
  51.4 4.7 %collective-permute-start = (bf16[32,128,128]{2,1,0:T(8,128)(2,1)S(1)}, bf16[32,128,128]{2,1,0:T(8,128)(2,1)S(1)}, u32[]{:S(2)}, u32[]{:S(2)}) collective-permute-start(bf16[32,128,128]{2,1,0:T(8,128)(2,1)S(1)} %all-to-all-done.mine_ref), channel_id=1, source_target_pairs={{0,48},{48,0},{1,49},{49,1},{2,50},{50,2},{3,51},{51,3},{4,52},{52... | collective-permute-start | bytes 3145736 | tf_op jit(solution)/shard_map/ppermute | solution.py:120

commit v3 on v2

v3 whole, which is shorter than its diff:
```python
import math

import jax
import jax.numpy as jnp
from jax import lax
from jax.experimental import pallas as pl
from jax.experimental.pallas import tpu as pltpu
from jax.sharding import Mesh
from jax.sharding import PartitionSpec as P

BS = 128
SLAB = 256
ORDER = 6144
FACTOR = 1.0 / math.sqrt(ORDER)
N_YL, N_X, N_CORE, N_Z, N_YH = 2, 4, 2, 12, 4
LIMIT = 24 * 1024 * 1024


def vmem(n):
    return [pl.BlockSpec(memory_space=pltpu.VMEM)] * n


def row_index():
    return (lax.axis_index("yl") * N_X + lax.axis_index("x")) * N_CORE + lax.axis_index("core")


def prepare(occ_hbm, values_hbm, slab_ref, mask_ref, send_hbm, occ_ref, values_ref, blocks_ref, in_sem, out_sem):
    copies = [
        pltpu.make_async_copy(occ_hbm, occ_ref, in_sem.at[0]),
        pltpu.make_async_copy(values_hbm, values_ref, in_sem.at[1]),
    ]
    for copy in copies:
        copy.start()
    for copy in copies:
        copy.wait()
    first = 3 * row_index()
    for q in range(N_YH):
        t = lax.rem(q + 4 * 48 - first, 4)
        held = jnp.minimum(t, 2)
        keep = jnp.where(t < 3, occ_ref[held], 0).astype(jnp.float32).astype(jnp.bfloat16)
        blocks_ref[q] = values_ref[pl.ds(pl.multiple_of(held * BS, BS), BS), :] * keep
    copies = [
        pltpu.make_async_copy(blocks_ref, send_hbm.at[pl.ds(j * N_YH, N_YH)], out_sem.at[j])
        for j in range(N_YL * N_X)
    ]
    for copy in copies:
        copy.start()
    for t in range(2):
        rows = pl.ds(t * BS, BS)
        keep = occ_ref[t].astype(jnp.float32)
        slab_ref[rows, :] = values_ref[rows, :] * keep.astype(jnp.bfloat16)
        mask_ref[t * 8:(t + 1) * 8, :] = jnp.full((8, BS), keep, jnp.float32)
    for copy in copies:
        copy.wait()


def assemble(s_ref, sk_ref):
    for z in range(N_Z):
        sk_ref[:, z * BS:(z + 1) * BS] = s_ref[z]


def first_product(s_ref, mine_ref, other_ref, out_ref, mk_ref, sk_ref):
    assemble(s_ref, sk_ref)
    my_core, yh = lax.axis_index("core"), lax.axis_index("yh")
    for z in range(N_Z):
        r = lax.div(4 * z + yh, 3)
        slot = lax.div(r, 2) * N_YH
        here = lax.rem(r, 2) == my_core

        @pl.when(here)
        def _():
            for q in range(N_YH):
                mk_ref[z * BS:(z + 1) * BS, q * BS:(q + 1) * BS] = mine_ref[slot + q]

        @pl.when(jnp.logical_not(here))
        def _():
            for q in range(N_YH):
                mk_ref[z * BS:(z + 1) * BS, q * BS:(q + 1) * BS] = other_ref[slot + q]

    total = jnp.dot(sk_ref[...], mk_ref[...], preferred_element_type=jnp.float32)
    for q in range(N_YH):
        out_ref[q] = total[:, q * BS:(q + 1) * BS]


def second_product(s_ref, mk_ref, out_ref, sk_ref):
    assemble(s_ref, sk_ref)
    total = jnp.dot(sk_ref[...], mk_ref[...], preferred_element_type=jnp.float32)
    for q in range(N_YH):
        out_ref[q] = total[:, q * BS:(q + 1) * BS]


def finish_square(mask_ref, parts_ref, out_ref):
    for t in range(2):
        rows = pl.ds(t * BS, BS)
        total = (parts_ref[0, rows, :] + parts_ref[1, rows, :]) + (parts_ref[2, rows, :] + parts_ref[3, rows, :])
        out_ref[rows, :] = (total * FACTOR * mask_ref[t * 8:t * 8 + 1, :]).astype(jnp.bfloat16)


def finish_sign(mask_ref, slab_ref, parts_ref, out_ref):
    for t in range(2):
        rows = pl.ds(t * BS, BS)
        total = (parts_ref[0, rows, :] + parts_ref[1, rows, :]) + (parts_ref[2, rows, :] + parts_ref[3, rows, :])
        step = 1.5 * slab_ref[rows, :].astype(jnp.float32) - 0.5 * FACTOR * total
        out_ref[rows, :] = (step * mask_ref[t * 8:t * 8 + 1, :]).astype(jnp.bfloat16)


def shape(*dims, dtype=jnp.bfloat16):
    return jax.ShapeDtypeStruct(dims, dtype)


def kernel(body, n_in, out_shape, scratch=(), flops=0, moved=1 << 20):
    return pl.pallas_call(
        body,
        out_shape=out_shape,
        in_specs=vmem(n_in),
        out_specs=jax.tree.map(lambda _: pl.BlockSpec(memory_space=pltpu.VMEM), out_shape),
        scratch_shapes=list(scratch),
        compiler_params=pltpu.CompilerParams(vmem_limit_bytes=LIMIT),
        cost_estimate=pl.CostEstimate(flops=flops, bytes_accessed=moved, transcendentals=0),
    )


def local(values, occupancy):
    group = N_YL * N_X * N_YH
    anywhere, in_vmem = pl.BlockSpec(memory_space=pl.ANY), pl.BlockSpec(memory_space=pltpu.VMEM)
    slab, mask, send = pl.pallas_call(
        prepare,
        out_shape=(shape(SLAB, BS), shape(16, BS, dtype=jnp.float32), shape(group, BS, BS)),
        in_specs=[anywhere, anywhere],
        out_specs=(in_vmem, in_vmem, anywhere),
        scratch_shapes=[
            pltpu.SMEM((3,), jnp.int32),
            pltpu.VMEM((3 * BS, BS), jnp.bfloat16),
            pltpu.VMEM((N_YH, BS, BS), jnp.bfloat16),
            pltpu.SemaphoreType.DMA((2,)),
            pltpu.SemaphoreType.DMA((N_YL * N_X,)),
        ],
        compiler_params=pltpu.CompilerParams(vmem_limit_bytes=60 * 1024 * 1024),
    )(occupancy.reshape(3), values)
    mine = lax.all_to_all(send, ("yl", "x", "yh"), 0, 0, tiled=True)
    gathered = lax.all_gather(slab, "z", axis=0, tiled=False)
    mine, gathered = lax.optimization_barrier((mine, gathered))
    other = lax.ppermute(mine, "core", [(0, 1), (1, 0)])
    cost = dict(flops=2 * SLAB * 12 * BS * 4 * BS, moved=4 << 20)
    sk = pltpu.VMEM((SLAB, N_Z * BS), jnp.bfloat16)
    parts_shape = shape(N_YH, SLAB, BS, dtype=jnp.float32)
    parts, mk = kernel(
        first_product, 3, (parts_shape, shape(N_Z * BS, N_YH * BS)), (sk,), **cost
    )(gathered, mine, other)
    parts = lax.all_to_all(parts, "yh", 0, 0, tiled=True)
    square_slab = kernel(finish_square, 2, shape(SLAB, BS))(mask, parts)
    gathered = lax.all_gather(square_slab, "z", axis=0, tiled=False)
    parts = kernel(second_product, 2, parts_shape, (sk,), **cost)(gathered, mk)
    parts = lax.all_to_all(parts, "yh", 0, 0, tiled=True)
    sign_step = kernel(finish_sign, 3, shape(SLAB, BS))(mask, slab, parts)
    return (square_slab, sign_step)


def solution(mesh):
    fine = Mesh(
        mesh.devices.reshape(N_YL, N_X, N_CORE, N_Z, N_YH), ("yl", "x", "core", "z", "yh")
    )
    spec = P(("yl", "x", "core"), ("z", "yh"))
    return jax.shard_map(local, mesh=fine, in_specs=(spec, spec), out_specs=(spec, spec), check_vma=False)
```

time: 126 us -> 123 us (0.976)
  local copies, waits for them, and re-layouts: 1.55 us -> 0.01 us
    unnamed x6 -> x4, local copies, waits for them, and re-layouts: 1.55 us -> 0.01 us
where the time goes in v3:
time: 123 us; the launch traced here: 122 us
  blocking collectives  97.7 us (79%)
  starting transfers between devices  15.3 us (12%)
  Pallas kernels  5.67 us (5%)
  waiting for transfers between devices  2.63 us (2%)
    all_to_all x2, blocking collectives, local(): parts = lax.all_to_all(parts, 'yh', 0, 0, tiled=True)  38.7 us
    all_gather x1, blocking collectives, local(): gathered = lax.all_gather(slab, 'z', axis=0, tiled=False)  34.4 us
    all_gather x1, blocking collectives, local(): gathered = lax.all_gather(square_slab, 'z', axis=0, tiled=False)  24.6 us
    all_to_all x1, starting transfers between devices, local(): mine = lax.all_to_all(send, ('yl', 'x', 'yh'), 0, 0, tiled=True)  13.3 us
    ppermute x1, waiting for transfers between devices, local(): other = lax.ppermute(mine, 'core', [(0, 1), (1, 0)])  2.63 us
    pallas_call x1, Pallas kernels, local(): pl.pallas_call(prepare, out_shape=(shape(SLAB, BS), shape(16, BS, dtype=j...  2.62 us
  transfers between devices with their start and end apart: 2, of which 1 were waited for; matrix products, arithmetic and copies ran while one was open for 0% of the time, Pallas kernels for 0%

profile of v3, /device:TPU:6, one launch (start us, length us, event | category | flops | bytes accessed | tf_op | source)
XLA Modules:
  0.0 122.0 jit_solution(5102270389839563894)
XLA Ops:
  0.6 2.6 %shard_map.41 = (bf16[256,128]{1,0:T(8,128)(2,1)}, f32[16,128]{1,0:T(8,128)}, bf16[32,128,128]{2,1,0:T(8,128)(2,1)}) custom-call(s32[3]{0:T(128)} %bitcast.5, bf16[384,128]{1,0:T(8,128)(2,1)} %values_hbm.1), custom_call_target="tpu_custom_call" | custom-call | tf_op jit(solution)/shard_map/pallas_call | solution.py:126
  3.3 0.0 copy-start
  3.3 13.3 %all-to-all-start = ((bf16[32,128,128]{2,1,0:T(8,128)(2,1)}), bf16[32,128,128]{2,1,0:T(8,128)(2,1)S(1)}, u32[]{:S(2)}, u32[]{:S(2)}) async-start(bf16[32,128,128]{2,1,0:T(8,128)(2,1)} %get-tuple-element.10), calls=%async_computation | async-start | bytes 2097152 | tf_op jit(solution)/shard_map/all_to_all | solution.py:140
  16.6 0.0 copy-done
  16.6 34.4 %all-gather = bf16[3072,128]{1,0:T(8,128)(2,1)S(1)} all-gather(bf16[256,128]{1,0:T(8,128)(2,1)S(1)} %copy-done), channel_id=2, replica_groups=mesh['yl'=2,'x'=4,'core'=2,'z'=12,'yh'=4] {'z'}, dimensions={0}, use_global_device_ids=true | all-gather | bytes 851968 | tf_op jit(solution)/shard_map/all_gather | solution.py:141
  50.9 0.0 all-to-all-done.mine_ref
  50.9 0.0 copy-start.1
  50.9 2.0 %collective-permute-start = (bf16[32,128,128]{2,1,0:T(8,128)(2,1)S(1)}, bf16[32,128,128]{2,1,0:T(8,128)(2,1)S(1)}, u32[]{:S(2)}, u32[]{:S(2)}) collective-permute-start(bf16[32,128,128]{2,1,0:T(8,128)(2,1)S(1)} %all-to-all-done.mine_ref), channel_id=1, source_target_pairs={{0,48},{48,0},{1,49},{49,1},{2,50},{50,2},{3,51},{51,3},{4,52},{52... | collective-permute-start | bytes 3145736 | tf_op jit(solution)/shard_map/ppermute | solution.py:143
  53.0 2.6 %collective-permute-done.other_ref = bf16[32,128,128]{2,1,0:T(8,128)(2,1)S(1)} collective-permute-done((bf16[32,128,128]{2,1,0:T(8,128)(2,1)S(1)}, bf16[32,128,128]{2,1,0:T(8,128)(2,1)S(1)}, u32[]{:S(2)}, u32[]{:S(2)}) %collective-permute-start) | collective-permute-done | bytes 1048608 | tf_op jit(solution)/shard_map/ppermute | solution.py:143
  55.6 1.1 shard_map.42
  56.8 23.0 %all_to_all.15.parts_ref = f32[4,256,128]{2,1,0:T(8,128)S(1)} all-to-all(f32[4,256,128]{2,1,0:T(8,128)S(1)} %get-tuple-element.14), channel_id=1, replica_groups=mesh['yl'=2,'x'=4,'core'=2,'z'=12,'yh'=4] {'yh'}, dimensions={0} | all-to-all | bytes 1048576 | tf_op jit(solution)/shard_map/all_to_all | solution.py:150
  79.8 0.0 copy-done.1
  79.8 0.7 shard_map.43
  80.4 24.6 %all-gather.1 = bf16[3072,128]{1,0:T(8,128)(2,1)S(1)} all-gather(bf16[256,128]{1,0:T(8,128)(2,1)} %shard_map.43), channel_id=3, replica_groups=mesh['yl'=2,'x'=4,'core'=2,'z'=12,'yh'=4] {'z'}, dimensions={0}, use_global_device_ids=true | all-gather | bytes 851968 | tf_op jit(solution)/shard_map/all_gather | solution.py:152
  105.1 0.6 shard_map.44
  105.7 15.7 %all_to_all.16.parts_ref = f32[4,256,128]{2,1,0:T(8,128)S(1)} all-to-all(f32[4,256,128]{2,1,0:T(8,128)S(1)} %shard_map.44), channel_id=1, replica_groups=mesh['yl'=2,'x'=4,'core'=2,'z'=12,'yh'=4] {'yh'}, dimensions={0} | all-to-all | bytes 1048576 | tf_op jit(solution)/shard_map/all_to_all | solution.py:154
  121.4 0.7 shard_map.45
Async XLA Ops:
  3.3 13.3 %copy-start = (bf16[256,128]{1,0:T(8,128)(2,1)S(1)}, bf16[256,128]{1,0:T(8,128)(2,1)}, u32[]{:S(2)}) copy-start(bf16[256,128]{1,0:T(8,128)(2,1)} %get-tuple-element.11.slab_ref) | copy-start | bytes 196612
  3.3 47.7 %all-to-all-start = ((bf16[32,128,128]{2,1,0:T(8,128)(2,1)}), bf16[32,128,128]{2,1,0:T(8,128)(2,1)S(1)}, u32[]{:S(2)}, u32[]{:S(2)}) async-start(bf16[32,128,128]{2,1,0:T(8,128)(2,1)} %get-tuple-element.10), calls=%async_computation | async-start | bytes 2097152 | tf_op jit(solution)/shard_map/all_to_all | solution.py:140
  50.9 28.8 %copy-start.1 = (f32[16,128]{1,0:T(8,128)S(1)}, f32[16,128]{1,0:T(8,128)}, u32[]{:S(2)}) copy-start(f32[16,128]{1,0:T(8,128)} %get-tuple-element.9.mask_ref) | copy-start | bytes 24580
  50.9 4.7 %collective-permute-start = (bf16[32,128,128]{2,1,0:T(8,128)(2,1)S(1)}, bf16[32,128,128]{2,1,0:T(8,128)(2,1)S(1)}, u32[]{:S(2)}, u32[]{:S(2)}) collective-permute-start(bf16[32,128,128]{2,1,0:T(8,128)(2,1)S(1)} %all-to-all-done.mine_ref), channel_id=1, source_target_pairs={{0,48},{48,0},{1,49},{49,1},{2,50},{50,2},{3,51},{51,3},{4,52},{52... | collective-permute-start | bytes 3145736 | tf_op jit(solution)/shard_map/ppermute | solution.py:143

commit v4 on v3

--- a/solution.py
+++ b/solution.py
@@ -13,6 +13,7 @@
 ORDER = 6144
 FACTOR = 1.0 / math.sqrt(ORDER)
 N_YL, N_X, N_CORE, N_Z, N_YH = 2, 4, 2, 12, 4
+N_GROUP = SLAB // 16
 LIMIT = 24 * 1024 * 1024
 
 
@@ -54,13 +55,38 @@
         copy.wait()
 
 
-def assemble(s_ref, sk_ref):
+def power_of_two(n, low):
+    result = jnp.full(n.shape, 2.0**low, jnp.float32)
+    for bit in range(7):
+        factor = jnp.where(((n - low) >> bit) & 1 == 1, jnp.float32(2.0 ** (2**bit)), jnp.float32(1.0))
+        result = result * factor
+    return result
+
+
+def encode(total):
+    groups = total.reshape(N_GROUP, 16, BS)
+    largest = jnp.max(jnp.abs(groups), axis=1)
+    exponent = jnp.floor(jnp.log2(jnp.maximum(largest, 2.0**-100))).astype(jnp.int32) + 1
+    scaled = groups * power_of_two(15 - exponent, -13)[:, None, :]
+    rounded = jnp.clip(jnp.floor(scaled + 0.5), -32767.0, 32767.0).astype(jnp.int32)
+    return rounded.reshape(SLAB, BS).astype(jnp.int16), exponent.astype(jnp.int16)
+
+
+def decode(parts_ref, q):
+    groups = parts_ref[q, :SLAB, :].astype(jnp.int32).astype(jnp.float32).reshape(N_GROUP, 16, BS)
+    scale = power_of_two(parts_ref[q, SLAB:, :].astype(jnp.int32) - 15, -115)
+    return (groups * scale[:, None, :]).reshape(SLAB, BS)
+
+
+def multiply(s_ref, sk_ref, mk_ref, out_ref):
     for z in range(N_Z):
         sk_ref[:, z * BS:(z + 1) * BS] = s_ref[z]
+    total = jnp.dot(sk_ref[...], mk_ref[...], preferred_element_type=jnp.float32)
+    for q in range(N_YH):
+        out_ref[q, :SLAB, :], out_ref[q, SLAB:, :] = encode(total[:, q * BS:(q + 1) * BS])
 
 
 def first_product(s_ref, mine_ref, other_ref, out_ref, mk_ref, sk_ref):
-    assemble(s_ref, sk_ref)
     my_core, yh = lax.axis_index("core"), lax.axis_index("yh")
     for z in range(N_Z):
         r = lax.div(4 * z + yh, 3)
@@ -77,30 +103,29 @@
             for q in range(N_YH):
                 mk_ref[z * BS:(z + 1) * BS, q * BS:(q + 1) * BS] = other_ref[slot + q]
 
-    total = jnp.dot(sk_ref[...], mk_ref[...], preferred_element_type=jnp.float32)
-    for q in range(N_YH):
-        out_ref[q] = total[:, q * BS:(q + 1) * BS]
+    multiply(s_ref, sk_ref, mk_ref, out_ref)
 
 
 def second_product(s_ref, mk_ref, out_ref, sk_ref):
-    assemble(s_ref, sk_ref)
-    total = jnp.dot(sk_ref[...], mk_ref[...], preferred_element_type=jnp.float32)
-    for q in range(N_YH):
-        out_ref[q] = total[:, q * BS:(q + 1) * BS]
+    multiply(s_ref, sk_ref, mk_ref, out_ref)
+
+
+def add_parts(parts_ref):
+    return (decode(parts_ref, 0) + decode(parts_ref, 1)) + (decode(parts_ref, 2) + decode(parts_ref, 3))
 
 
 def finish_square(mask_ref, parts_ref, out_ref):
+    total = add_parts(parts_ref)
     for t in range(2):
-        rows = pl.ds(t * BS, BS)
-        total = (parts_ref[0, rows, :] + parts_ref[1, rows, :]) + (parts_ref[2, rows, :] + parts_ref[3, rows, :])
-        out_ref[rows, :] = (total * FACTOR * mask_ref[t * 8:t * 8 + 1, :]).astype(jnp.bfloat16)
+        rows = slice(t * BS, (t + 1) * BS)
+        out_ref[rows, :] = (total[rows] * FACTOR * mask_ref[t * 8:t * 8 + 1, :]).astype(jnp.bfloat16)
 
 
 def finish_sign(mask_ref, slab_ref, parts_ref, out_ref):
+    total = add_parts(parts_ref)
     for t in range(2):
-        rows = pl.ds(t * BS, BS)
-        total = (parts_ref[0, rows, :] + parts_ref[1, rows, :]) + (parts_ref[2, rows, :] + parts_ref[3, rows, :])
-        step = 1.5 * slab_ref[rows, :].astype(jnp.float32) - 0.5 * FACTOR * total
+        rows = slice(t * BS, (t + 1) * BS)
+        step = 1.5 * slab_ref[rows, :].astype(jnp.float32) - 0.5 * FACTOR * total[rows]
         out_ref[rows, :] = (step * mask_ref[t * 8:t * 8 + 1, :]).astype(jnp.bfloat16)
 
 
@@ -143,7 +168,7 @@
     other = lax.ppermute(mine, "core", [(0, 1), (1, 0)])
     cost = dict(flops=2 * SLAB * 12 * BS * 4 * BS, moved=4 << 20)
     sk = pltpu.VMEM((SLAB, N_Z * BS), jnp.bfloat16)
-    parts_shape = shape(N_YH, SLAB, BS, dtype=jnp.float32)
+    parts_shape = shape(N_YH, SLAB + N_GROUP, BS, dtype=jnp.int16)
     parts, mk = kernel(
         first_product, 3, (parts_shape, shape(N_Z * BS, N_YH * BS)), (sk,), **cost
     )(gathered, mine, other)

time: 123 us -> 117 us (0.951)
  blocking collectives: 97.7 us -> 90.8 us
    all_to_all x2, blocking collectives: 38.7 us -> 31.2 us  [local(): parts = lax.all_to_all(parts, 'yh', 0, 0, tiled=True)]
where the time goes in v4:
time: 117 us; the launch traced here: 116 us
  blocking collectives  90.8 us (78%)
  starting transfers between devices  15.3 us (13%)
  Pallas kernels  6.83 us (6%)
  waiting for transfers between devices  2.63 us (2%)
    all_gather x1, blocking collectives, local(): gathered = lax.all_gather(slab, 'z', axis=0, tiled=False)  34.4 us
    all_to_all x2, blocking collectives, local(): parts = lax.all_to_all(parts, 'yh', 0, 0, tiled=True)  31.2 us
    all_gather x1, blocking collectives, local(): gathered = lax.all_gather(square_slab, 'z', axis=0, tiled=False)  25.2 us
    all_to_all x1, starting transfers between devices, local(): mine = lax.all_to_all(send, ('yl', 'x', 'yh'), 0, 0, tiled=True)  13.3 us
    ppermute x1, waiting for transfers between devices, local(): other = lax.ppermute(mine, 'core', [(0, 1), (1, 0)])  2.63 us
    pallas_call x1, Pallas kernels, local(): pl.pallas_call(prepare, out_shape=(shape(SLAB, BS), shape(16, BS, dtype=j...  2.62 us
  transfers between devices with their start and end apart: 2, of which 1 were waited for; matrix products, arithmetic and copies ran while one was open for 0% of the time, Pallas kernels for 0%

profile of v4, /device:TPU:6, one launch (start us, length us, event | category | flops | bytes accessed | tf_op | source)
XLA Modules:
  0.0 116.3 jit_solution(16910946039384526469)
XLA Ops:
  0.6 2.6 %shard_map.41 = (bf16[256,128]{1,0:T(8,128)(2,1)}, f32[16,128]{1,0:T(8,128)}, bf16[32,128,128]{2,1,0:T(8,128)(2,1)}) custom-call(s32[3]{0:T(128)} %bitcast.5, bf16[384,128]{1,0:T(8,128)(2,1)} %values_hbm.1), custom_call_target="tpu_custom_call" | custom-call | tf_op jit(solution)/shard_map/pallas_call | solution.py:151
  3.3 0.0 copy-start
  3.3 13.3 %all-to-all-start = ((bf16[32,128,128]{2,1,0:T(8,128)(2,1)}), bf16[32,128,128]{2,1,0:T(8,128)(2,1)S(1)}, u32[]{:S(2)}, u32[]{:S(2)}) async-start(bf16[32,128,128]{2,1,0:T(8,128)(2,1)} %get-tuple-element.10), calls=%async_computation | async-start | bytes 2097152 | tf_op jit(solution)/shard_map/all_to_all | solution.py:165
  16.6 0.0 copy-done
  16.6 34.4 %all-gather = bf16[3072,128]{1,0:T(8,128)(2,1)S(1)} all-gather(bf16[256,128]{1,0:T(8,128)(2,1)S(1)} %copy-done), channel_id=2, replica_groups=mesh['yl'=2,'x'=4,'core'=2,'z'=12,'yh'=4] {'z'}, dimensions={0}, use_global_device_ids=true | all-gather | bytes 851968 | tf_op jit(solution)/shard_map/all_gather | solution.py:166
  50.9 0.0 all-to-all-done.mine_ref
  50.9 0.0 copy-start.1
  50.9 2.0 %collective-permute-start = (bf16[32,128,128]{2,1,0:T(8,128)(2,1)S(1)}, bf16[32,128,128]{2,1,0:T(8,128)(2,1)S(1)}, u32[]{:S(2)}, u32[]{:S(2)}) collective-permute-start(bf16[32,128,128]{2,1,0:T(8,128)(2,1)S(1)} %all-to-all-done.mine_ref), channel_id=1, source_target_pairs={{0,48},{48,0},{1,49},{49,1},{2,50},{50,2},{3,51},{51,3},{4,52},{52... | collective-permute-start | bytes 3145736 | tf_op jit(solution)/shard_map/ppermute | solution.py:168
  53.0 2.6 %collective-permute-done.other_ref = bf16[32,128,128]{2,1,0:T(8,128)(2,1)S(1)} collective-permute-done((bf16[32,128,128]{2,1,0:T(8,128)(2,1)S(1)}, bf16[32,128,128]{2,1,0:T(8,128)(2,1)S(1)}, u32[]{:S(2)}, u32[]{:S(2)}) %collective-permute-start) | collective-permute-done | bytes 1048608 | tf_op jit(solution)/shard_map/ppermute | solution.py:168
  55.6 1.5 %shard_map.42 = (s16[4,272,128]{2,1,0:T(8,128)(2,1)S(1)}, bf16[1536,512]{1,0:T(8,128)(2,1)S(1)}) custom-call(bf16[12,256,128]{2,1,0:T(8,128)(2,1)S(1)} %bitcast.3, bf16[32,128,128]{2,1,0:T(8,128)(2,1)S(1)} %all-to-all-done.mine_ref, bf16[32,128,128]{2,1,0:T(8,128)(2,1)S(1)} %collective-permute-done.other_ref), custom_call_target="tpu_custom_call" | custom-call | flops 402653184 | bytes 4194304 | tf_op jit(solution)/shard_map/pallas_call | solution.py:172
  57.2 18.2 %all_to_all.15.parts_ref = s16[4,272,128]{2,1,0:T(8,128)(2,1)S(1)} all-to-all(s16[4,272,128]{2,1,0:T(8,128)(2,1)S(1)} %get-tuple-element.14), channel_id=1, replica_groups=mesh['yl'=2,'x'=4,'core'=2,'z'=12,'yh'=4] {'yh'}, dimensions={0} | all-to-all | bytes 557056 | tf_op jit(solution)/shard_map/all_to_all | solution.py:175
  75.4 0.0 copy-done.1
  75.4 0.8 shard_map.43
  76.2 25.2 %all-gather.1 = bf16[3072,128]{1,0:T(8,128)(2,1)S(1)} all-gather(bf16[256,128]{1,0:T(8,128)(2,1)} %shard_map.43), channel_id=3, replica_groups=mesh['yl'=2,'x'=4,'core'=2,'z'=12,'yh'=4] {'z'}, dimensions={0}, use_global_device_ids=true | all-gather | bytes 851968 | tf_op jit(solution)/shard_map/all_gather | solution.py:177
  101.3 1.1 shard_map.44
  102.5 13.0 %all_to_all.16.parts_ref = s16[4,272,128]{2,1,0:T(8,128)(2,1)S(1)} all-to-all(s16[4,272,128]{2,1,0:T(8,128)(2,1)S(1)} %shard_map.44), channel_id=1, replica_groups=mesh['yl'=2,'x'=4,'core'=2,'z'=12,'yh'=4] {'yh'}, dimensions={0} | all-to-all | bytes 557056 | tf_op jit(solution)/shard_map/all_to_all | solution.py:179
  115.5 0.8 shard_map.45
Async XLA Ops:
  3.3 13.3 %copy-start = (bf16[256,128]{1,0:T(8,128)(2,1)S(1)}, bf16[256,128]{1,0:T(8,128)(2,1)}, u32[]{:S(2)}) copy-start(bf16[256,128]{1,0:T(8,128)(2,1)} %get-tuple-element.11.slab_ref) | copy-start | bytes 196612
  3.3 47.7 %all-to-all-start = ((bf16[32,128,128]{2,1,0:T(8,128)(2,1)}), bf16[32,128,128]{2,1,0:T(8,128)(2,1)S(1)}, u32[]{:S(2)}, u32[]{:S(2)}) async-start(bf16[32,128,128]{2,1,0:T(8,128)(2,1)} %get-tuple-element.10), calls=%async_computation | async-start | bytes 2097152 | tf_op jit(solution)/shard_map/all_to_all | solution.py:165
  50.9 24.4 %copy-start.1 = (f32[16,128]{1,0:T(8,128)S(1)}, f32[16,128]{1,0:T(8,128)}, u32[]{:S(2)}) copy-start(f32[16,128]{1,0:T(8,128)} %get-tuple-element.9.mask_ref) | copy-start | bytes 24580
  50.9 4.7 %collective-permute-start = (bf16[32,128,128]{2,1,0:T(8,128)(2,1)S(1)}, bf16[32,128,128]{2,1,0:T(8,128)(2,1)S(1)}, u32[]{:S(2)}, u32[]{:S(2)}) collective-permute-start(bf16[32,128,128]{2,1,0:T(8,128)(2,1)S(1)} %all-to-all-done.mine_ref), channel_id=1, source_target_pairs={{0,48},{48,0},{1,49},{49,1},{2,50},{50,2},{3,51},{51,3},{4,52},{52... | collective-permute-start | bytes 3145736 | tf_op jit(solution)/shard_map/ppermute | solution.py:168

commit v5 on v4

--- a/solution.py
+++ b/solution.py
@@ -78,15 +78,13 @@
     return (groups * scale[:, None, :]).reshape(SLAB, BS)
 
 
-def multiply(s_ref, sk_ref, mk_ref, out_ref):
-    for z in range(N_Z):
-        sk_ref[:, z * BS:(z + 1) * BS] = s_ref[z]
-    total = jnp.dot(sk_ref[...], mk_ref[...], preferred_element_type=jnp.float32)
+def multiply(s_ref, mk_ref, out_ref):
+    total = jnp.dot(s_ref[...], mk_ref[...], preferred_element_type=jnp.float32)
     for q in range(N_YH):
         out_ref[q, :SLAB, :], out_ref[q, SLAB:, :] = encode(total[:, q * BS:(q + 1) * BS])
 
 
-def first_product(s_ref, mine_ref, other_ref, out_ref, mk_ref, sk_ref):
+def first_product(s_ref, mine_ref, other_ref, out_ref, mk_ref):
     my_core, yh = lax.axis_index("core"), lax.axis_index("yh")
     for z in range(N_Z):
         r = lax.div(4 * z + yh, 3)
@@ -103,11 +101,11 @@
             for q in range(N_YH):
                 mk_ref[z * BS:(z + 1) * BS, q * BS:(q + 1) * BS] = other_ref[slot + q]
 
-    multiply(s_ref, sk_ref, mk_ref, out_ref)
+    multiply(s_ref, mk_ref, out_ref)
 
 
-def second_product(s_ref, mk_ref, out_ref, sk_ref):
-    multiply(s_ref, sk_ref, mk_ref, out_ref)
+def second_product(s_ref, mk_ref, out_ref):
+    multiply(s_ref, mk_ref, out_ref)
 
 
 def add_parts(parts_ref):
@@ -133,13 +131,12 @@
     return jax.ShapeDtypeStruct(dims, dtype)
 
 
-def kernel(body, n_in, out_shape, scratch=(), flops=0, moved=1 << 20):
+def kernel(body, n_in, out_shape, flops=0, moved=1 << 20):
     return pl.pallas_call(
         body,
         out_shape=out_shape,
         in_specs=vmem(n_in),
         out_specs=jax.tree.map(lambda _: pl.BlockSpec(memory_space=pltpu.VMEM), out_shape),
-        scratch_shapes=list(scratch),
         compiler_params=pltpu.CompilerParams(vmem_limit_bytes=LIMIT),
         cost_estimate=pl.CostEstimate(flops=flops, bytes_accessed=moved, transcendentals=0),
     )
@@ -163,19 +160,17 @@
         compiler_params=pltpu.CompilerParams(vmem_limit_bytes=60 * 1024 * 1024),
     )(occupancy.reshape(3), values)
     mine = lax.all_to_all(send, ("yl", "x", "yh"), 0, 0, tiled=True)
-    gathered = lax.all_gather(slab, "z", axis=0, tiled=False)
+    gathered = lax.all_gather(slab, "z", axis=1, tiled=True)
     mine, gathered = lax.optimization_barrier((mine, gathered))
     other = lax.ppermute(mine, "core", [(0, 1), (1, 0)])
     cost = dict(flops=2 * SLAB * 12 * BS * 4 * BS, moved=4 << 20)
-    sk = pltpu.VMEM((SLAB, N_Z * BS), jnp.bfloat16)
     parts_shape = shape(N_YH, SLAB + N_GROUP, BS, dtype=jnp.int16)
-    parts, mk = kernel(
-        first_product, 3, (parts_shape, shape(N_Z * BS, N_YH * BS)), (sk,), **cost
-    )(gathered, mine, other)
+    mk_shape = shape(N_Z * BS, N_YH * BS)
+    parts, mk = kernel(first_product, 3, (parts_shape, mk_shape), **cost)(gathered, mine, other)
     parts = lax.all_to_all(parts, "yh", 0, 0, tiled=True)
     square_slab = kernel(finish_square, 2, shape(SLAB, BS))(mask, parts)
-    gathered = lax.all_gather(square_slab, "z", axis=0, tiled=False)
-    parts = kernel(second_product, 2, parts_shape, (sk,), **cost)(gathered, mk)
+    gathered = lax.all_gather(square_slab, "z", axis=1, tiled=True)
+    parts = kernel(second_product, 2, parts_shape, **cost)(gathered, mk)
     parts = lax.all_to_all(parts, "yh", 0, 0, tiled=True)
     sign_step = kernel(finish_sign, 3, shape(SLAB, BS))(mask, slab, parts)
     return (square_slab, sign_step)

time: 117 us -> 117 us (level)
  no operation moved by 1% of the time
where the time goes in v5:
time: 117 us; the launch traced here: 116 us
  blocking collectives  90.8 us (78%)
  starting transfers between devices  15.3 us (13%)
  Pallas kernels  6.79 us (6%)
  waiting for transfers between devices  2.63 us (2%)
    all_gather x1, blocking collectives, local(): gathered = lax.all_gather(slab, 'z', axis=1, tiled=True)  34.4 us
    all_to_all x2, blocking collectives, local(): parts = lax.all_to_all(parts, 'yh', 0, 0, tiled=True)  31.2 us
    all_gather x1, blocking collectives, local(): gathered = lax.all_gather(square_slab, 'z', axis=1, tiled=True)  25.2 us
    all_to_all x1, starting transfers between devices, local(): mine = lax.all_to_all(send, ('yl', 'x', 'yh'), 0, 0, tiled=True)  13.3 us
    ppermute x1, waiting for transfers between devices, local(): other = lax.ppermute(mine, 'core', [(0, 1), (1, 0)])  2.63 us
    pallas_call x1, Pallas kernels, local(): pl.pallas_call(prepare, out_shape=(shape(SLAB, BS), shape(16, BS, dtype=j...  2.62 us
  transfers between devices with their start and end apart: 2, of which 1 were waited for; matrix products, arithmetic and copies ran while one was open for 0% of the time, Pallas kernels for 0%

profile of v5, /device:TPU:6, one launch (start us, length us, event | category | flops | bytes accessed | tf_op | source)
XLA Modules:
  0.0 116.2 jit_solution(17203199235156206333)
XLA Ops:
  0.6 2.6 %shard_map.41 = (bf16[256,128]{1,0:T(8,128)(2,1)}, f32[16,128]{1,0:T(8,128)}, bf16[32,128,128]{2,1,0:T(8,128)(2,1)}) custom-call(s32[3]{0:T(128)} %bitcast.1, bf16[384,128]{1,0:T(8,128)(2,1)} %values_hbm.1), custom_call_target="tpu_custom_call" | custom-call | tf_op jit(solution)/shard_map/pallas_call | solution.py:148
  3.3 0.0 copy-start
  3.3 13.3 %all-to-all-start = ((bf16[32,128,128]{2,1,0:T(8,128)(2,1)}), bf16[32,128,128]{2,1,0:T(8,128)(2,1)S(1)}, u32[]{:S(2)}, u32[]{:S(2)}) async-start(bf16[32,128,128]{2,1,0:T(8,128)(2,1)} %get-tuple-element.10), calls=%async_computation | async-start | bytes 2097152 | tf_op jit(solution)/shard_map/all_to_all | solution.py:162
  16.6 0.0 copy-done
  16.6 34.4 %all_gather.6.s_ref = bf16[256,1536]{1,0:T(8,128)(2,1)S(1)} all-gather(bf16[256,128]{1,0:T(8,128)(2,1)S(1)} %copy-done), channel_id=1, replica_groups=mesh['yl'=2,'x'=4,'core'=2,'z'=12,'yh'=4] {'z'}, dimensions={1}, use_global_device_ids=true | all-gather | bytes 851968 | tf_op jit(solution)/shard_map/all_gather | solution.py:163
  50.9 0.0 copy-start.1
  50.9 0.0 all-to-all-done.mine_ref
  50.9 2.0 %collective-permute-start = (bf16[32,128,128]{2,1,0:T(8,128)(2,1)S(1)}, bf16[32,128,128]{2,1,0:T(8,128)(2,1)S(1)}, u32[]{:S(2)}, u32[]{:S(2)}) collective-permute-start(bf16[32,128,128]{2,1,0:T(8,128)(2,1)S(1)} %all-to-all-done.mine_ref), channel_id=1, source_target_pairs={{0,48},{48,0},{1,49},{49,1},{2,50},{50,2},{3,51},{51,3},{4,52},{52... | collective-permute-start | bytes 3145736 | tf_op jit(solution)/shard_map/ppermute | solution.py:165
  53.0 2.6 %collective-permute-done.other_ref = bf16[32,128,128]{2,1,0:T(8,128)(2,1)S(1)} collective-permute-done((bf16[32,128,128]{2,1,0:T(8,128)(2,1)S(1)}, bf16[32,128,128]{2,1,0:T(8,128)(2,1)S(1)}, u32[]{:S(2)}, u32[]{:S(2)}) %collective-permute-start) | collective-permute-done | bytes 1048608 | tf_op jit(solution)/shard_map/ppermute | solution.py:165
  55.6 1.5 %shard_map.42 = (s16[4,272,128]{2,1,0:T(8,128)(2,1)S(1)}, bf16[1536,512]{1,0:T(8,128)(2,1)S(1)}) custom-call(bf16[256,1536]{1,0:T(8,128)(2,1)S(1)} %all_gather.6.s_ref, bf16[32,128,128]{2,1,0:T(8,128)(2,1)S(1)} %all-to-all-done.mine_ref, bf16[32,128,128]{2,1,0:T(8,128)(2,1)S(1)} %collective-permute-done.other_ref), custom_call_target="tpu_custom_call" | custom-call | flops 402653184 | bytes 4194304 | tf_op jit(solution)/shard_map/pallas_call | solution.py:169
  57.1 18.2 %all_to_all.15.parts_ref = s16[4,272,128]{2,1,0:T(8,128)(2,1)S(1)} all-to-all(s16[4,272,128]{2,1,0:T(8,128)(2,1)S(1)} %get-tuple-element.14), channel_id=1, replica_groups=mesh['yl'=2,'x'=4,'core'=2,'z'=12,'yh'=4] {'yh'}, dimensions={0} | all-to-all | bytes 557056 | tf_op jit(solution)/shard_map/all_to_all | solution.py:170
  75.4 0.0 copy-done.1
  75.4 0.8 shard_map.43
  76.1 25.2 %all_gather.7.s_ref = bf16[256,1536]{1,0:T(8,128)(2,1)S(1)} all-gather(bf16[256,128]{1,0:T(8,128)(2,1)} %shard_map.43), channel_id=1, replica_groups=mesh['yl'=2,'x'=4,'core'=2,'z'=12,'yh'=4] {'z'}, dimensions={1}, use_global_device_ids=true | all-gather | bytes 851968 | tf_op jit(solution)/shard_map/all_gather | solution.py:172
  101.3 1.1 shard_map.44
  102.4 13.0 %all_to_all.16.parts_ref = s16[4,272,128]{2,1,0:T(8,128)(2,1)S(1)} all-to-all(s16[4,272,128]{2,1,0:T(8,128)(2,1)S(1)} %shard_map.44), channel_id=1, replica_groups=mesh['yl'=2,'x'=4,'core'=2,'z'=12,'yh'=4] {'yh'}, dimensions={0} | all-to-all | bytes 557056 | tf_op jit(solution)/shard_map/all_to_all | solution.py:174
  115.4 0.8 shard_map.45
Async XLA Ops:
  3.3 13.3 %copy-start = (bf16[256,128]{1,0:T(8,128)(2,1)S(1)}, bf16[256,128]{1,0:T(8,128)(2,1)}, u32[]{:S(2)}) copy-start(bf16[256,128]{1,0:T(8,128)(2,1)} %get-tuple-element.11.slab_ref) | copy-start | bytes 196612
  3.3 47.7 %all-to-all-start = ((bf16[32,128,128]{2,1,0:T(8,128)(2,1)}), bf16[32,128,128]{2,1,0:T(8,128)(2,1)S(1)}, u32[]{:S(2)}, u32[]{:S(2)}) async-start(bf16[32,128,128]{2,1,0:T(8,128)(2,1)} %get-tuple-element.10), calls=%async_computation | async-start | bytes 2097152 | tf_op jit(solution)/shard_map/all_to_all | solution.py:162
  50.9 24.4 %copy-start.1 = (f32[16,128]{1,0:T(8,128)S(1)}, f32[16,128]{1,0:T(8,128)}, u32[]{:S(2)}) copy-start(f32[16,128]{1,0:T(8,128)} %get-tuple-element.9.mask_ref) | copy-start | bytes 24580
  50.9 4.7 %collective-permute-start = (bf16[32,128,128]{2,1,0:T(8,128)(2,1)S(1)}, bf16[32,128,128]{2,1,0:T(8,128)(2,1)S(1)}, u32[]{:S(2)}, u32[]{:S(2)}) collective-permute-start(bf16[32,128,128]{2,1,0:T(8,128)(2,1)S(1)} %all-to-all-done.mine_ref), channel_id=1, source_target_pairs={{0,48},{48,0},{1,49},{49,1},{2,50},{50,2},{3,51},{51,3},{4,52},{52... | collective-permute-start | bytes 3145736 | tf_op jit(solution)/shard_map/ppermute | solution.py:165

commit v6 on v5

--- a/solution.py
+++ b/solution.py
@@ -25,33 +25,39 @@
     return (lax.axis_index("yl") * N_X + lax.axis_index("x")) * N_CORE + lax.axis_index("core")
 
 
-def prepare(occ_hbm, values_hbm, slab_ref, mask_ref, send_hbm, occ_ref, values_ref, blocks_ref, in_sem, out_sem):
-    copies = [
+def prepare(
+    occ_hbm, values_hbm, slab_hbm, mask_hbm, send_hbm,
+    occ_ref, values_ref, slab_ref, mask_ref, blocks_ref, in_sem, out_sem, send_sem,
+):
+    read = [
         pltpu.make_async_copy(occ_hbm, occ_ref, in_sem.at[0]),
         pltpu.make_async_copy(values_hbm, values_ref, in_sem.at[1]),
     ]
-    for copy in copies:
+    for copy in read:
         copy.start()
-    for copy in copies:
+    for copy in read:
         copy.wait()
+    written = []
     first = 3 * row_index()
     for q in range(N_YH):
         t = lax.rem(q + 4 * 48 - first, 4)
         held = jnp.minimum(t, 2)
         keep = jnp.where(t < 3, occ_ref[held], 0).astype(jnp.float32).astype(jnp.bfloat16)
         blocks_ref[q] = values_ref[pl.ds(pl.multiple_of(held * BS, BS), BS), :] * keep
-    copies = [
-        pltpu.make_async_copy(blocks_ref, send_hbm.at[pl.ds(j * N_YH, N_YH)], out_sem.at[j])
-        for j in range(N_YL * N_X)
-    ]
-    for copy in copies:
+    for j in range(N_YL * N_X):
+        copy = pltpu.make_async_copy(blocks_ref, send_hbm.at[pl.ds(j * N_YH, N_YH)], send_sem.at[j])
         copy.start()
+        written.append(copy)
     for t in range(2):
         rows = pl.ds(t * BS, BS)
         keep = occ_ref[t].astype(jnp.float32)
         slab_ref[rows, :] = values_ref[rows, :] * keep.astype(jnp.bfloat16)
         mask_ref[t * 8:(t + 1) * 8, :] = jnp.full((8, BS), keep, jnp.float32)
-    for copy in copies:
+    for i, (source, target) in enumerate(((slab_ref, slab_hbm), (mask_ref, mask_hbm))):
+        copy = pltpu.make_async_copy(source, target, out_sem.at[i])
+        copy.start()
+        written.append(copy)
+    for copy in written:
         copy.wait()
 
 
@@ -144,16 +150,19 @@
 
 def local(values, occupancy):
     group = N_YL * N_X * N_YH
-    anywhere, in_vmem = pl.BlockSpec(memory_space=pl.ANY), pl.BlockSpec(memory_space=pltpu.VMEM)
+    anywhere = pl.BlockSpec(memory_space=pl.ANY)
     slab, mask, send = pl.pallas_call(
         prepare,
         out_shape=(shape(SLAB, BS), shape(16, BS, dtype=jnp.float32), shape(group, BS, BS)),
         in_specs=[anywhere, anywhere],
-        out_specs=(in_vmem, in_vmem, anywhere),
+        out_specs=(anywhere, anywhere, anywhere),
         scratch_shapes=[
             pltpu.SMEM((3,), jnp.int32),
             pltpu.VMEM((3 * BS, BS), jnp.bfloat16),
+            pltpu.VMEM((SLAB, BS), jnp.bfloat16),
+            pltpu.VMEM((16, BS), jnp.float32),
             pltpu.VMEM((N_YH, BS, BS), jnp.bfloat16),
+            pltpu.SemaphoreType.DMA((2,)),
             pltpu.SemaphoreType.DMA((2,)),
             pltpu.SemaphoreType.DMA((N_YL * N_X,)),
         ],

time: 117 us -> 116 us (level)
  no operation moved by 1% of the time
where the time goes in v6:
time: 116 us
  blocking collectives  90.8 us (78%)
  starting transfers between devices  15.3 us (13%)
  Pallas kernels  6.18 us (5%)
  waiting for transfers between devices  2.63 us (2%)
    all_gather x1, blocking collectives, local(): gathered = lax.all_gather(slab, 'z', axis=1, tiled=True)  34.4 us
    all_to_all x2, blocking collectives, local(): parts = lax.all_to_all(parts, 'yh', 0, 0, tiled=True)  31.2 us
    all_gather x1, blocking collectives, local(): gathered = lax.all_gather(square_slab, 'z', axis=1, tiled=True)  25.2 us
    all_to_all x1, starting transfers between devices, local(): mine = lax.all_to_all(send, ('yl', 'x', 'yh'), 0, 0, tiled=True)  13.3 us
    ppermute x1, waiting for transfers between devices, local(): other = lax.ppermute(mine, 'core', [(0, 1), (1, 0)])  2.63 us
  transfers between devices with their start and end apart: 2, of which 1 were waited for; matrix products, arithmetic and copies ran while one was open for 0% of the time, Pallas kernels for 0%

profile of v6, /device:TPU:6, one launch (start us, length us, event | category | flops | bytes accessed | tf_op | source)
XLA Modules:
  0.0 115.6 jit_solution(7071198367236275853)
XLA Ops:
  0.6 2.0 %shard_map.41 = (bf16[256,128]{1,0:T(8,128)(2,1)}, f32[16,128]{1,0:T(8,128)}, bf16[32,128,128]{2,1,0:T(8,128)(2,1)}) custom-call(s32[3]{0:T(128)} %bitcast.1, bf16[384,128]{1,0:T(8,128)(2,1)} %values_hbm.1), custom_call_target="tpu_custom_call" | custom-call | tf_op jit(solution)/shard_map/pallas_call | solution.py:154
  2.6 0.0 copy-start
  2.7 13.3 %all-to-all-start = ((bf16[32,128,128]{2,1,0:T(8,128)(2,1)}), bf16[32,128,128]{2,1,0:T(8,128)(2,1)S(1)}, u32[]{:S(2)}, u32[]{:S(2)}) async-start(bf16[32,128,128]{2,1,0:T(8,128)(2,1)} %get-tuple-element.10), calls=%async_computation | async-start | bytes 2097152 | tf_op jit(solution)/shard_map/all_to_all | solution.py:171
  16.0 0.0 copy-done
  16.0 34.4 %all_gather.6.s_ref = bf16[256,1536]{1,0:T(8,128)(2,1)S(1)} all-gather(bf16[256,128]{1,0:T(8,128)(2,1)S(1)} %copy-done), channel_id=1, replica_groups=mesh['yl'=2,'x'=4,'core'=2,'z'=12,'yh'=4] {'z'}, dimensions={1}, use_global_device_ids=true | all-gather | bytes 851968 | tf_op jit(solution)/shard_map/all_gather | solution.py:172
  50.3 0.0 copy-start.1
  50.3 0.0 all-to-all-done.mine_ref
  50.3 2.0 %collective-permute-start = (bf16[32,128,128]{2,1,0:T(8,128)(2,1)S(1)}, bf16[32,128,128]{2,1,0:T(8,128)(2,1)S(1)}, u32[]{:S(2)}, u32[]{:S(2)}) collective-permute-start(bf16[32,128,128]{2,1,0:T(8,128)(2,1)S(1)} %all-to-all-done.mine_ref), channel_id=1, source_target_pairs={{0,48},{48,0},{1,49},{49,1},{2,50},{50,2},{3,51},{51,3},{4,52},{52... | collective-permute-start | bytes 3145736 | tf_op jit(solution)/shard_map/ppermute | solution.py:174
  52.4 2.6 %collective-permute-done.other_ref = bf16[32,128,128]{2,1,0:T(8,128)(2,1)S(1)} collective-permute-done((bf16[32,128,128]{2,1,0:T(8,128)(2,1)S(1)}, bf16[32,128,128]{2,1,0:T(8,128)(2,1)S(1)}, u32[]{:S(2)}, u32[]{:S(2)}) %collective-permute-start) | collective-permute-done | bytes 1048608 | tf_op jit(solution)/shard_map/ppermute | solution.py:174
  55.0 1.5 %shard_map.42 = (s16[4,272,128]{2,1,0:T(8,128)(2,1)S(1)}, bf16[1536,512]{1,0:T(8,128)(2,1)S(1)}) custom-call(bf16[256,1536]{1,0:T(8,128)(2,1)S(1)} %all_gather.6.s_ref, bf16[32,128,128]{2,1,0:T(8,128)(2,1)S(1)} %all-to-all-done.mine_ref, bf16[32,128,128]{2,1,0:T(8,128)(2,1)S(1)} %collective-permute-done.other_ref), custom_call_target="tpu_custom_call" | custom-call | flops 402653184 | bytes 4194304 | tf_op jit(solution)/shard_map/pallas_call | solution.py:178
  56.5 18.2 %all_to_all.15.parts_ref = s16[4,272,128]{2,1,0:T(8,128)(2,1)S(1)} all-to-all(s16[4,272,128]{2,1,0:T(8,128)(2,1)S(1)} %get-tuple-element.14), channel_id=1, replica_groups=mesh['yl'=2,'x'=4,'core'=2,'z'=12,'yh'=4] {'yh'}, dimensions={0} | all-to-all | bytes 557056 | tf_op jit(solution)/shard_map/all_to_all | solution.py:179
  74.7 0.0 copy-done.1
  74.8 0.8 shard_map.43
  75.5 25.2 %all_gather.7.s_ref = bf16[256,1536]{1,0:T(8,128)(2,1)S(1)} all-gather(bf16[256,128]{1,0:T(8,128)(2,1)} %shard_map.43), channel_id=1, replica_groups=mesh['yl'=2,'x'=4,'core'=2,'z'=12,'yh'=4] {'z'}, dimensions={1}, use_global_device_ids=true | all-gather | bytes 851968 | tf_op jit(solution)/shard_map/all_gather | solution.py:181
  100.7 1.1 shard_map.44
  101.8 13.0 %all_to_all.16.parts_ref = s16[4,272,128]{2,1,0:T(8,128)(2,1)S(1)} all-to-all(s16[4,272,128]{2,1,0:T(8,128)(2,1)S(1)} %shard_map.44), channel_id=1, replica_groups=mesh['yl'=2,'x'=4,'core'=2,'z'=12,'yh'=4] {'yh'}, dimensions={0} | all-to-all | bytes 557056 | tf_op jit(solution)/shard_map/all_to_all | solution.py:183
  114.8 0.8 shard_map.45
Async XLA Ops:
  2.6 13.3 %copy-start = (bf16[256,128]{1,0:T(8,128)(2,1)S(1)}, bf16[256,128]{1,0:T(8,128)(2,1)}, u32[]{:S(2)}) copy-start(bf16[256,128]{1,0:T(8,128)(2,1)} %get-tuple-element.11.slab_ref) | copy-start | bytes 196612
  2.7 47.7 %all-to-all-start = ((bf16[32,128,128]{2,1,0:T(8,128)(2,1)}), bf16[32,128,128]{2,1,0:T(8,128)(2,1)S(1)}, u32[]{:S(2)}, u32[]{:S(2)}) async-start(bf16[32,128,128]{2,1,0:T(8,128)(2,1)} %get-tuple-element.10), calls=%async_computation | async-start | bytes 2097152 | tf_op jit(solution)/shard_map/all_to_all | solution.py:171
  50.3 24.4 %copy-start.1 = (f32[16,128]{1,0:T(8,128)S(1)}, f32[16,128]{1,0:T(8,128)}, u32[]{:S(2)}) copy-start(f32[16,128]{1,0:T(8,128)} %get-tuple-element.9.mask_ref) | copy-start | bytes 24580
  50.3 4.7 %collective-permute-start = (bf16[32,128,128]{2,1,0:T(8,128)(2,1)S(1)}, bf16[32,128,128]{2,1,0:T(8,128)(2,1)S(1)}, u32[]{:S(2)}, u32[]{:S(2)}) collective-permute-start(bf16[32,128,128]{2,1,0:T(8,128)(2,1)S(1)} %all-to-all-done.mine_ref), channel_id=1, source_target_pairs={{0,48},{48,0},{1,49},{49,1},{2,50},{50,2},{3,51},{51,3},{4,52},{52... | collective-permute-start | bytes 3145736 | tf_op jit(solution)/shard_map/ppermute | solution.py:174

commit v7 on v6

--- a/solution.py
+++ b/solution.py
@@ -110,8 +110,11 @@
     multiply(s_ref, mk_ref, out_ref)
 
 
-def second_product(s_ref, mk_ref, out_ref):
+def second_product(s_ref, mk_ref, square_ref, out_ref, square_hbm, sem):
+    copy = pltpu.make_async_copy(square_ref, square_hbm, sem)
+    copy.start()
     multiply(s_ref, mk_ref, out_ref)
+    copy.wait()
 
 
 def add_parts(parts_ref):
@@ -177,9 +180,17 @@
     mk_shape = shape(N_Z * BS, N_YH * BS)
     parts, mk = kernel(first_product, 3, (parts_shape, mk_shape), **cost)(gathered, mine, other)
     parts = lax.all_to_all(parts, "yh", 0, 0, tiled=True)
-    square_slab = kernel(finish_square, 2, shape(SLAB, BS))(mask, parts)
-    gathered = lax.all_gather(square_slab, "z", axis=1, tiled=True)
-    parts = kernel(second_product, 2, parts_shape, **cost)(gathered, mk)
+    square = kernel(finish_square, 2, shape(SLAB, BS))(mask, parts)
+    gathered = lax.all_gather(square, "z", axis=1, tiled=True)
+    parts, square_slab = pl.pallas_call(
+        second_product,
+        out_shape=(parts_shape, shape(SLAB, BS)),
+        in_specs=vmem(3),
+        out_specs=(pl.BlockSpec(memory_space=pltpu.VMEM), anywhere),
+        scratch_shapes=[pltpu.SemaphoreType.DMA],
+        compiler_params=pltpu.CompilerParams(vmem_limit_bytes=LIMIT),
+        cost_estimate=pl.CostEstimate(flops=cost["flops"], bytes_accessed=cost["moved"], transcendentals=0),
+    )(gathered, mk, square)
     parts = lax.all_to_all(parts, "yh", 0, 0, tiled=True)
     sign_step = kernel(finish_sign, 3, shape(SLAB, BS))(mask, slab, parts)
     return (square_slab, sign_step)

time: 116 us -> 115 us (level)
  no operation moved by 1% of the time
where the time goes in v7:
time: 115 us
  blocking collectives  90.6 us (79%)
  starting transfers between devices  15.3 us (13%)
  Pallas kernels  5.56 us (5%)
  waiting for transfers between devices  2.63 us (2%)
    all_gather x1, blocking collectives, local(): gathered = lax.all_gather(slab, 'z', axis=1, tiled=True)  34.4 us
    all_to_all x2, blocking collectives, local(): parts = lax.all_to_all(parts, 'yh', 0, 0, tiled=True)  31.1 us
    all_gather x1, blocking collectives, local(): gathered = lax.all_gather(square, 'z', axis=1, tiled=True)  25.1 us
    all_to_all x1, starting transfers between devices, local(): mine = lax.all_to_all(send, ('yl', 'x', 'yh'), 0, 0, tiled=True)  13.3 us
    ppermute x1, waiting for transfers between devices, local(): other = lax.ppermute(mine, 'core', [(0, 1), (1, 0)])  2.63 us
  transfers between devices with their start and end apart: 2, of which 1 were waited for; matrix products, arithmetic and copies ran while one was open for 0% of the time, Pallas kernels for 0%

profile of v7, /device:TPU:6, one launch (start us, length us, event | category | flops | bytes accessed | tf_op | source)
XLA Modules:
  0.0 114.8 jit_solution(5254416212433178219)
XLA Ops:
  0.6 2.0 %shard_map.41 = (bf16[256,128]{1,0:T(8,128)(2,1)}, f32[16,128]{1,0:T(8,128)}, bf16[32,128,128]{2,1,0:T(8,128)(2,1)}) custom-call(s32[3]{0:T(128)} %bitcast.1, bf16[384,128]{1,0:T(8,128)(2,1)} %values_hbm.1), custom_call_target="tpu_custom_call" | custom-call | tf_op jit(solution)/shard_map/pallas_call | solution.py:157
  2.6 0.0 copy-start
  2.7 13.3 %all-to-all-start = ((bf16[32,128,128]{2,1,0:T(8,128)(2,1)}), bf16[32,128,128]{2,1,0:T(8,128)(2,1)S(1)}, u32[]{:S(2)}, u32[]{:S(2)}) async-start(bf16[32,128,128]{2,1,0:T(8,128)(2,1)} %get-tuple-element.12), calls=%async_computation | async-start | bytes 2097152 | tf_op jit(solution)/shard_map/all_to_all | solution.py:174
  16.0 0.0 copy-done
  16.0 34.4 %all_gather.6.s_ref = bf16[256,1536]{1,0:T(8,128)(2,1)S(1)} all-gather(bf16[256,128]{1,0:T(8,128)(2,1)S(1)} %copy-done), channel_id=1, replica_groups=mesh['yl'=2,'x'=4,'core'=2,'z'=12,'yh'=4] {'z'}, dimensions={1}, use_global_device_ids=true | all-gather | bytes 851968 | tf_op jit(solution)/shard_map/all_gather | solution.py:175
  50.3 0.0 copy-start.1
  50.3 0.0 all-to-all-done.mine_ref
  50.3 2.0 %collective-permute-start = (bf16[32,128,128]{2,1,0:T(8,128)(2,1)S(1)}, bf16[32,128,128]{2,1,0:T(8,128)(2,1)S(1)}, u32[]{:S(2)}, u32[]{:S(2)}) collective-permute-start(bf16[32,128,128]{2,1,0:T(8,128)(2,1)S(1)} %all-to-all-done.mine_ref), channel_id=1, source_target_pairs={{0,48},{48,0},{1,49},{49,1},{2,50},{50,2},{3,51},{51,3},{4,52},{52... | collective-permute-start | bytes 3145736 | tf_op jit(solution)/shard_map/ppermute | solution.py:177
  52.4 2.6 %collective-permute-done.other_ref = bf16[32,128,128]{2,1,0:T(8,128)(2,1)S(1)} collective-permute-done((bf16[32,128,128]{2,1,0:T(8,128)(2,1)S(1)}, bf16[32,128,128]{2,1,0:T(8,128)(2,1)S(1)}, u32[]{:S(2)}, u32[]{:S(2)}) %collective-permute-start) | collective-permute-done | bytes 1048608 | tf_op jit(solution)/shard_map/ppermute | solution.py:177
  55.0 1.5 %shard_map.42 = (s16[4,272,128]{2,1,0:T(8,128)(2,1)S(1)}, bf16[1536,512]{1,0:T(8,128)(2,1)S(1)}) custom-call(bf16[256,1536]{1,0:T(8,128)(2,1)S(1)} %all_gather.6.s_ref, bf16[32,128,128]{2,1,0:T(8,128)(2,1)S(1)} %all-to-all-done.mine_ref, bf16[32,128,128]{2,1,0:T(8,128)(2,1)S(1)} %collective-permute-done.other_ref), custom_call_target="tpu_custom_call" | custom-call | flops 402653184 | bytes 4194304 | tf_op jit(solution)/shard_map/pallas_call | solution.py:181
  56.5 18.2 %all_to_all.15.parts_ref = s16[4,272,128]{2,1,0:T(8,128)(2,1)S(1)} all-to-all(s16[4,272,128]{2,1,0:T(8,128)(2,1)S(1)} %get-tuple-element.16), channel_id=1, replica_groups=mesh['yl'=2,'x'=4,'core'=2,'z'=12,'yh'=4] {'yh'}, dimensions={0} | all-to-all | bytes 557056 | tf_op jit(solution)/shard_map/all_to_all | solution.py:182
  74.7 0.0 copy-done.1
  74.7 0.1 shard_map.43.square_ref
  74.9 25.1 %all_gather.7.s_ref = bf16[256,1536]{1,0:T(8,128)(2,1)S(1)} all-gather(bf16[256,128]{1,0:T(8,128)(2,1)S(1)} %shard_map.43.square_ref), channel_id=1, replica_groups=mesh['yl'=2,'x'=4,'core'=2,'z'=12,'yh'=4] {'z'}, dimensions={1}, use_global_device_ids=true | all-gather | bytes 851968 | tf_op jit(solution)/shard_map/all_gather | solution.py:184
  100.0 1.1 shard_map.44
  101.1 12.9 %all_to_all.16.parts_ref = s16[4,272,128]{2,1,0:T(8,128)(2,1)S(1)} all-to-all(s16[4,272,128]{2,1,0:T(8,128)(2,1)S(1)} %get-tuple-element.19), channel_id=1, replica_groups=mesh['yl'=2,'x'=4,'core'=2,'z'=12,'yh'=4] {'yh'}, dimensions={0} | all-to-all | bytes 557056 | tf_op jit(solution)/shard_map/all_to_all | solution.py:194
  114.1 0.8 shard_map.45
Async XLA Ops:
  2.6 13.3 %copy-start = (bf16[256,128]{1,0:T(8,128)(2,1)S(1)}, bf16[256,128]{1,0:T(8,128)(2,1)}, u32[]{:S(2)}) copy-start(bf16[256,128]{1,0:T(8,128)(2,1)} %get-tuple-element.13.slab_ref) | copy-start | bytes 196612
  2.7 47.7 %all-to-all-start = ((bf16[32,128,128]{2,1,0:T(8,128)(2,1)}), bf16[32,128,128]{2,1,0:T(8,128)(2,1)S(1)}, u32[]{:S(2)}, u32[]{:S(2)}) async-start(bf16[32,128,128]{2,1,0:T(8,128)(2,1)} %get-tuple-element.12), calls=%async_computation | async-start | bytes 2097152 | tf_op jit(solution)/shard_map/all_to_all | solution.py:174
  50.3 24.4 %copy-start.1 = (f32[16,128]{1,0:T(8,128)S(1)}, f32[16,128]{1,0:T(8,128)}, u32[]{:S(2)}) copy-start(f32[16,128]{1,0:T(8,128)} %get-tuple-element.11.mask_ref) | copy-start | bytes 24580
  50.3 4.7 %collective-permute-start = (bf16[32,128,128]{2,1,0:T(8,128)(2,1)S(1)}, bf16[32,128,128]{2,1,0:T(8,128)(2,1)S(1)}, u32[]{:S(2)}, u32[]{:S(2)}) collective-permute-start(bf16[32,128,128]{2,1,0:T(8,128)(2,1)S(1)} %all-to-all-done.mine_ref), channel_id=1, source_target_pairs={{0,48},{48,0},{1,49},{49,1},{2,50},{50,2},{3,51},{51,3},{4,52},{52... | collective-permute-start | bytes 3145736 | tf_op jit(solution)/shard_map/ppermute | solution.py:177

commit v8 on v7

--- a/solution.py
+++ b/solution.py
@@ -14,6 +14,7 @@
 FACTOR = 1.0 / math.sqrt(ORDER)
 N_YL, N_X, N_CORE, N_Z, N_YH = 2, 4, 2, 12, 4
 N_GROUP = SLAB // 16
+PLACES = [2, 3, 0, 1]
 LIMIT = 24 * 1024 * 1024
 
 
@@ -87,7 +88,8 @@
 def multiply(s_ref, mk_ref, out_ref):
     total = jnp.dot(s_ref[...], mk_ref[...], preferred_element_type=jnp.float32)
     for q in range(N_YH):
-        out_ref[q, :SLAB, :], out_ref[q, SLAB:, :] = encode(total[:, q * BS:(q + 1) * BS])
+        at = PLACES.index(q)
+        out_ref[at, :SLAB, :], out_ref[at, SLAB:, :] = encode(total[:, q * BS:(q + 1) * BS])
 
 
 def first_product(s_ref, mine_ref, other_ref, out_ref, mk_ref):
@@ -179,7 +181,7 @@
     parts_shape = shape(N_YH, SLAB + N_GROUP, BS, dtype=jnp.int16)
     mk_shape = shape(N_Z * BS, N_YH * BS)
     parts, mk = kernel(first_product, 3, (parts_shape, mk_shape), **cost)(gathered, mine, other)
-    parts = lax.all_to_all(parts, "yh", 0, 0, tiled=True)
+    parts = lax.all_to_all(parts, "yh", 0, 0, tiled=True, axis_index_groups=[PLACES])
     square = kernel(finish_square, 2, shape(SLAB, BS))(mask, parts)
     gathered = lax.all_gather(square, "z", axis=1, tiled=True)
     parts, square_slab = pl.pallas_call(
@@ -191,7 +193,7 @@
         compiler_params=pltpu.CompilerParams(vmem_limit_bytes=LIMIT),
         cost_estimate=pl.CostEstimate(flops=cost["flops"], bytes_accessed=cost["moved"], transcendentals=0),
     )(gathered, mk, square)
-    parts = lax.all_to_all(parts, "yh", 0, 0, tiled=True)
+    parts = lax.all_to_all(parts, "yh", 0, 0, tiled=True, axis_index_groups=[PLACES])
     sign_step = kernel(finish_sign, 3, shape(SLAB, BS))(mask, slab, parts)
     return (square_slab, sign_step)
 

time: 115 us -> 113 us (0.983); the launches traced: 115 us -> 111 us
  blocking collectives: 90.6 us -> 87.2 us
    all_to_all x2, blocking collectives: 31.1 us -> 27.6 us  [local(): lax.all_to_all(parts, 'yh', 0, 0, tiled=True, axis_index_groups=[PLACES])]
where the time goes in v8:
time: 113 us; the launch traced here: 111 us
  blocking collectives  87.2 us (77%)
  starting transfers between devices  15.3 us (14%)
  Pallas kernels  5.56 us (5%)
  waiting for transfers between devices  2.63 us (2%)
    all_gather x1, blocking collectives, local(): gathered = lax.all_gather(slab, 'z', axis=1, tiled=True)  34.4 us
    all_to_all x2, blocking collectives, local(): lax.all_to_all(parts, 'yh', 0, 0, tiled=True, axis_index_groups=[PLACES])  27.6 us
    all_gather x1, blocking collectives, local(): gathered = lax.all_gather(square, 'z', axis=1, tiled=True)  25.2 us
    all_to_all x1, starting transfers between devices, local(): mine = lax.all_to_all(send, ('yl', 'x', 'yh'), 0, 0, tiled=True)  13.3 us
    ppermute x1, waiting for transfers between devices, local(): other = lax.ppermute(mine, 'core', [(0, 1), (1, 0)])  2.63 us
  transfers between devices with their start and end apart: 2, of which 1 were waited for; matrix products, arithmetic and copies ran while one was open for 0% of the time, Pallas kernels for 0%

profile of v8, /device:TPU:6, one launch (start us, length us, event | category | flops | bytes accessed | tf_op | source)
XLA Modules:
  0.0 111.4 jit_solution(13774387271754858058)
XLA Ops:
  0.6 2.0 %shard_map.41 = (bf16[256,128]{1,0:T(8,128)(2,1)}, f32[16,128]{1,0:T(8,128)}, bf16[32,128,128]{2,1,0:T(8,128)(2,1)}) custom-call(s32[3]{0:T(128)} %bitcast.1, bf16[384,128]{1,0:T(8,128)(2,1)} %values_hbm.1), custom_call_target="tpu_custom_call" | custom-call | tf_op jit(solution)/shard_map/pallas_call | solution.py:159
  2.6 0.0 copy-start
  2.7 13.3 %all-to-all-start = ((bf16[32,128,128]{2,1,0:T(8,128)(2,1)}), bf16[32,128,128]{2,1,0:T(8,128)(2,1)S(1)}, u32[]{:S(2)}, u32[]{:S(2)}) async-start(bf16[32,128,128]{2,1,0:T(8,128)(2,1)} %get-tuple-element.12), calls=%async_computation | async-start | bytes 2097152 | tf_op jit(solution)/shard_map/all_to_all | solution.py:176
  16.0 0.0 copy-done
  16.0 34.4 %all_gather.6.s_ref = bf16[256,1536]{1,0:T(8,128)(2,1)S(1)} all-gather(bf16[256,128]{1,0:T(8,128)(2,1)S(1)} %copy-done), channel_id=1, replica_groups=mesh['yl'=2,'x'=4,'core'=2,'z'=12,'yh'=4] {'z'}, dimensions={1}, use_global_device_ids=true | all-gather | bytes 851968 | tf_op jit(solution)/shard_map/all_gather | solution.py:177
  50.3 0.0 copy-start.1
  50.3 0.0 all-to-all-done.mine_ref
  50.3 2.0 %collective-permute-start = (bf16[32,128,128]{2,1,0:T(8,128)(2,1)S(1)}, bf16[32,128,128]{2,1,0:T(8,128)(2,1)S(1)}, u32[]{:S(2)}, u32[]{:S(2)}) collective-permute-start(bf16[32,128,128]{2,1,0:T(8,128)(2,1)S(1)} %all-to-all-done.mine_ref), channel_id=1, source_target_pairs={{0,48},{48,0},{1,49},{49,1},{2,50},{50,2},{3,51},{51,3},{4,52},{52... | collective-permute-start | bytes 3145736 | tf_op jit(solution)/shard_map/ppermute | solution.py:179
  52.4 2.6 %collective-permute-done.other_ref = bf16[32,128,128]{2,1,0:T(8,128)(2,1)S(1)} collective-permute-done((bf16[32,128,128]{2,1,0:T(8,128)(2,1)S(1)}, bf16[32,128,128]{2,1,0:T(8,128)(2,1)S(1)}, u32[]{:S(2)}, u32[]{:S(2)}) %collective-permute-start) | collective-permute-done | bytes 1048608 | tf_op jit(solution)/shard_map/ppermute | solution.py:179
  55.0 1.5 %shard_map.42 = (s16[4,272,128]{2,1,0:T(8,128)(2,1)S(1)}, bf16[1536,512]{1,0:T(8,128)(2,1)S(1)}) custom-call(bf16[256,1536]{1,0:T(8,128)(2,1)S(1)} %all_gather.6.s_ref, bf16[32,128,128]{2,1,0:T(8,128)(2,1)S(1)} %all-to-all-done.mine_ref, bf16[32,128,128]{2,1,0:T(8,128)(2,1)S(1)} %collective-permute-done.other_ref), custom_call_target="tpu_custom_call" | custom-call | flops 402653184 | bytes 4194304 | tf_op jit(solution)/shard_map/pallas_call | solution.py:183
  56.5 15.0 %all_to_all.15.parts_ref = s16[4,272,128]{2,1,0:T(8,128)(2,1)S(1)} all-to-all(s16[4,272,128]{2,1,0:T(8,128)(2,1)S(1)} %get-tuple-element.16), channel_id=1, replica_groups={{2,3,0,1},{6,7,4,5},{10,11,8,9},{14,15,12,13},{18,19,16,17},{22,23,20,2..., dimensions={0} | all-to-all | bytes 557056 | tf_op jit(solution)/shard_map/all_to_all | solution.py:184
  71.6 0.0 copy-done.1
  71.6 0.1 shard_map.43.square_ref
  71.7 25.2 %all_gather.7.s_ref = bf16[256,1536]{1,0:T(8,128)(2,1)S(1)} all-gather(bf16[256,128]{1,0:T(8,128)(2,1)S(1)} %shard_map.43.square_ref), channel_id=1, replica_groups=mesh['yl'=2,'x'=4,'core'=2,'z'=12,'yh'=4] {'z'}, dimensions={1}, use_global_device_ids=true | all-gather | bytes 851968 | tf_op jit(solution)/shard_map/all_gather | solution.py:186
  96.9 1.1 shard_map.44
  98.1 12.5 %all_to_all.16.parts_ref = s16[4,272,128]{2,1,0:T(8,128)(2,1)S(1)} all-to-all(s16[4,272,128]{2,1,0:T(8,128)(2,1)S(1)} %get-tuple-element.19), channel_id=1, replica_groups={{2,3,0,1},{6,7,4,5},{10,11,8,9},{14,15,12,13},{18,19,16,17},{22,23,20,2..., dimensions={0} | all-to-all | bytes 557056 | tf_op jit(solution)/shard_map/all_to_all | solution.py:196
  110.6 0.8 shard_map.45
Async XLA Ops:
  2.6 13.3 %copy-start = (bf16[256,128]{1,0:T(8,128)(2,1)S(1)}, bf16[256,128]{1,0:T(8,128)(2,1)}, u32[]{:S(2)}) copy-start(bf16[256,128]{1,0:T(8,128)(2,1)} %get-tuple-element.13.slab_ref) | copy-start | bytes 196612
  2.7 47.7 %all-to-all-start = ((bf16[32,128,128]{2,1,0:T(8,128)(2,1)}), bf16[32,128,128]{2,1,0:T(8,128)(2,1)S(1)}, u32[]{:S(2)}, u32[]{:S(2)}) async-start(bf16[32,128,128]{2,1,0:T(8,128)(2,1)} %get-tuple-element.12), calls=%async_computation | async-start | bytes 2097152 | tf_op jit(solution)/shard_map/all_to_all | solution.py:176
  50.3 21.2 %copy-start.1 = (f32[16,128]{1,0:T(8,128)S(1)}, f32[16,128]{1,0:T(8,128)}, u32[]{:S(2)}) copy-start(f32[16,128]{1,0:T(8,128)} %get-tuple-element.11.mask_ref) | copy-start | bytes 24580
  50.3 4.7 %collective-permute-start = (bf16[32,128,128]{2,1,0:T(8,128)(2,1)S(1)}, bf16[32,128,128]{2,1,0:T(8,128)(2,1)S(1)}, u32[]{:S(2)}, u32[]{:S(2)}) collective-permute-start(bf16[32,128,128]{2,1,0:T(8,128)(2,1)S(1)} %all-to-all-done.mine_ref), channel_id=1, source_target_pairs={{0,48},{48,0},{1,49},{49,1},{2,50},{50,2},{3,51},{51,3},{4,52},{52... | collective-permute-start | bytes 3145736 | tf_op jit(solution)/shard_map/ppermute | solution.py:179

commit v9 on v8

--- a/solution.py
+++ b/solution.py
@@ -15,6 +15,10 @@
 N_YL, N_X, N_CORE, N_Z, N_YH = 2, 4, 2, 12, 4
 N_GROUP = SLAB // 16
 PLACES = [2, 3, 0, 1]
+FIRST_PLACES = [3, 0, 1, 2]
+SECOND_PLACES = [2, 3, 0, 1]
+X_PLACES = [2, 3, 0, 1]
+YL_PLACES = [0, 1]
 LIMIT = 24 * 1024 * 1024
 
 
@@ -44,7 +48,7 @@
         t = lax.rem(q + 4 * 48 - first, 4)
         held = jnp.minimum(t, 2)
         keep = jnp.where(t < 3, occ_ref[held], 0).astype(jnp.float32).astype(jnp.bfloat16)
-        blocks_ref[q] = values_ref[pl.ds(pl.multiple_of(held * BS, BS), BS), :] * keep
+        blocks_ref[PLACES.index(q)] = values_ref[pl.ds(pl.multiple_of(held * BS, BS), BS), :] * keep
     for j in range(N_YL * N_X):
         copy = pltpu.make_async_copy(blocks_ref, send_hbm.at[pl.ds(j * N_YH, N_YH)], send_sem.at[j])
         copy.start()
@@ -85,37 +89,42 @@
     return (groups * scale[:, None, :]).reshape(SLAB, BS)
 
 
-def multiply(s_ref, mk_ref, out_ref):
+def multiply(s_ref, mk_ref, out_ref, places):
     total = jnp.dot(s_ref[...], mk_ref[...], preferred_element_type=jnp.float32)
     for q in range(N_YH):
-        at = PLACES.index(q)
+        at = places.index(q)
         out_ref[at, :SLAB, :], out_ref[at, SLAB:, :] = encode(total[:, q * BS:(q + 1) * BS])
+
+
+def place_of(chip):
+    yl, x = lax.div(chip, N_X), lax.rem(chip, N_X)
+    return lax.rem(yl + YL_PLACES[0], N_YL) * N_X + lax.rem(x + N_X - X_PLACES[0], N_X)
 
 
 def first_product(s_ref, mine_ref, other_ref, out_ref, mk_ref):
     my_core, yh = lax.axis_index("core"), lax.axis_index("yh")
     for z in range(N_Z):
         r = lax.div(4 * z + yh, 3)
-        slot = lax.div(r, 2) * N_YH
+        slot = place_of(lax.div(r, 2)) * N_YH
         here = lax.rem(r, 2) == my_core
 
         @pl.when(here)
         def _():
             for q in range(N_YH):
-                mk_ref[z * BS:(z + 1) * BS, q * BS:(q + 1) * BS] = mine_ref[slot + q]
+                mk_ref[z * BS:(z + 1) * BS, q * BS:(q + 1) * BS] = mine_ref[slot + PLACES.index(q)]
 
         @pl.when(jnp.logical_not(here))
         def _():
             for q in range(N_YH):
-                mk_ref[z * BS:(z + 1) * BS, q * BS:(q + 1) * BS] = other_ref[slot + q]
-
-    multiply(s_ref, mk_ref, out_ref)
+                mk_ref[z * BS:(z + 1) * BS, q * BS:(q + 1) * BS] = other_ref[slot + PLACES.index(q)]
+
+    multiply(s_ref, mk_ref, out_ref, FIRST_PLACES)
 
 
 def second_product(s_ref, mk_ref, square_ref, out_ref, square_hbm, sem):
     copy = pltpu.make_async_copy(square_ref, square_hbm, sem)
     copy.start()
-    multiply(s_ref, mk_ref, out_ref)
+    multiply(s_ref, mk_ref, out_ref, SECOND_PLACES)
     copy.wait()
 
 
@@ -155,6 +164,7 @@
 
 def local(values, occupancy):
     group = N_YL * N_X * N_YH
+    order = [(yl * N_X + x) * N_YH + yh for yl in YL_PLACES for x in X_PLACES for yh in PLACES]
     anywhere = pl.BlockSpec(memory_space=pl.ANY)
     slab, mask, send = pl.pallas_call(
         prepare,
@@ -173,7 +183,7 @@
         ],
         compiler_params=pltpu.CompilerParams(vmem_limit_bytes=60 * 1024 * 1024),
     )(occupancy.reshape(3), values)
-    mine = lax.all_to_all(send, ("yl", "x", "yh"), 0, 0, tiled=True)
+    mine = lax.all_to_all(send, ("yl", "x", "yh"), 0, 0, tiled=True, axis_index_groups=[order])
     gathered = lax.all_gather(slab, "z", axis=1, tiled=True)
     mine, gathered = lax.optimization_barrier((mine, gathered))
     other = lax.ppermute(mine, "core", [(0, 1), (1, 0)])
@@ -181,7 +191,7 @@
     parts_shape = shape(N_YH, SLAB + N_GROUP, BS, dtype=jnp.int16)
     mk_shape = shape(N_Z * BS, N_YH * BS)
     parts, mk = kernel(first_product, 3, (parts_shape, mk_shape), **cost)(gathered, mine, other)
-    parts = lax.all_to_all(parts, "yh", 0, 0, tiled=True, axis_index_groups=[PLACES])
+    parts = lax.all_to_all(parts, "yh", 0, 0, tiled=True, axis_index_groups=[FIRST_PLACES])
     square = kernel(finish_square, 2, shape(SLAB, BS))(mask, parts)
     gathered = lax.all_gather(square, "z", axis=1, tiled=True)
     parts, square_slab = pl.pallas_call(
@@ -193,7 +203,7 @@
         compiler_params=pltpu.CompilerParams(vmem_limit_bytes=LIMIT),
         cost_estimate=pl.CostEstimate(flops=cost["flops"], bytes_accessed=cost["moved"], transcendentals=0),
     )(gathered, mk, square)
-    parts = lax.all_to_all(parts, "yh", 0, 0, tiled=True, axis_index_groups=[PLACES])
+    parts = lax.all_to_all(parts, "yh", 0, 0, tiled=True, axis_index_groups=[SECOND_PLACES])
     sign_step = kernel(finish_sign, 3, shape(SLAB, BS))(mask, slab, parts)
     return (square_slab, sign_step)
 

time: 113 us -> 112 us (level)
  blocking collectives: 87.2 us -> 82.2 us
  starting transfers between devices: 15.3 us -> 18.8 us
    all_gather x1, blocking collectives: 34.4 us -> 30.4 us  [local(): gathered = lax.all_gather(slab, 'z', axis=1, tiled=True)]
    all_to_all x1, starting transfers between devices: 13.3 us -> 16.7 us  [local(): lax.all_to_all(send, ('yl', 'x', 'yh'), 0, 0, tiled=True, axis_index_grou...]
where the time goes in v9:
time: 112 us; the launch traced here: 110 us
  blocking collectives  82.2 us (73%)
  starting transfers between devices  18.8 us (17%)
  Pallas kernels  5.62 us (5%)
  waiting for transfers between devices  2.63 us (2%)
    all_gather x1, blocking collectives, local(): gathered = lax.all_gather(slab, 'z', axis=1, tiled=True)  30.4 us
    all_gather x1, blocking collectives, local(): gathered = lax.all_gather(square, 'z', axis=1, tiled=True)  25.3 us
    all_to_all x1, starting transfers between devices, local(): lax.all_to_all(send, ('yl', 'x', 'yh'), 0, 0, tiled=True, axis_index_grou...  16.7 us
    all_to_all x1, blocking collectives, local(): lax.all_to_all(parts, 'yh', 0, 0, tiled=True, axis_index_groups=[FIRST_PL...  14.2 us
    all_to_all x1, blocking collectives, local(): lax.all_to_all(parts, 'yh', 0, 0, tiled=True, axis_index_groups=[SECOND_P...  12.3 us
    ppermute x1, waiting for transfers between devices, local(): other = lax.ppermute(mine, 'core', [(0, 1), (1, 0)])  2.63 us
  transfers between devices with their start and end apart: 2, of which 1 were waited for; matrix products, arithmetic and copies ran while one was open for 0% of the time, Pallas kernels for 0%

profile of v9, /device:TPU:6, one launch (start us, length us, event | category | flops | bytes accessed | tf_op | source)
XLA Modules:
  0.0 109.9 jit_solution(17702698955414959435)
XLA Ops:
  0.6 2.0 %shard_map.41 = (bf16[256,128]{1,0:T(8,128)(2,1)}, f32[16,128]{1,0:T(8,128)}, bf16[32,128,128]{2,1,0:T(8,128)(2,1)}) custom-call(s32[3]{0:T(128)} %bitcast.1, bf16[384,128]{1,0:T(8,128)(2,1)} %values_hbm.1), custom_call_target="tpu_custom_call" | custom-call | tf_op jit(solution)/shard_map/pallas_call | solution.py:169
  2.6 0.0 copy-start
  2.7 16.7 %all-to-all-start = ((bf16[32,128,128]{2,1,0:T(8,128)(2,1)}), bf16[32,128,128]{2,1,0:T(8,128)(2,1)S(1)}, u32[]{:S(2)}, u32[]{:S(2)}) async-start(bf16[32,128,128]{2,1,0:T(8,128)(2,1)} %get-tuple-element.12), calls=%async_computation | async-start | bytes 2097152 | tf_op jit(solution)/shard_map/all_to_all | solution.py:186
  19.4 0.0 copy-done
  19.4 30.4 %all_gather.6.s_ref = bf16[256,1536]{1,0:T(8,128)(2,1)S(1)} all-gather(bf16[256,128]{1,0:T(8,128)(2,1)S(1)} %copy-done), channel_id=1, replica_groups=mesh['yl'=2,'x'=4,'core'=2,'z'=12,'yh'=4] {'z'}, dimensions={1}, use_global_device_ids=true | all-gather | bytes 851968 | tf_op jit(solution)/shard_map/all_gather | solution.py:187
  49.8 0.0 copy-start.1
  49.8 0.0 all-to-all-done.mine_ref
  49.8 2.0 %collective-permute-start = (bf16[32,128,128]{2,1,0:T(8,128)(2,1)S(1)}, bf16[32,128,128]{2,1,0:T(8,128)(2,1)S(1)}, u32[]{:S(2)}, u32[]{:S(2)}) collective-permute-start(bf16[32,128,128]{2,1,0:T(8,128)(2,1)S(1)} %all-to-all-done.mine_ref), channel_id=1, source_target_pairs={{0,48},{48,0},{1,49},{49,1},{2,50},{50,2},{3,51},{51,3},{4,52},{52... | collective-permute-start | bytes 3145736 | tf_op jit(solution)/shard_map/ppermute | solution.py:189
  51.9 2.6 %collective-permute-done.other_ref = bf16[32,128,128]{2,1,0:T(8,128)(2,1)S(1)} collective-permute-done((bf16[32,128,128]{2,1,0:T(8,128)(2,1)S(1)}, bf16[32,128,128]{2,1,0:T(8,128)(2,1)S(1)}, u32[]{:S(2)}, u32[]{:S(2)}) %collective-permute-start) | collective-permute-done | bytes 1048608 | tf_op jit(solution)/shard_map/ppermute | solution.py:189
  54.5 1.6 %shard_map.42 = (s16[4,272,128]{2,1,0:T(8,128)(2,1)S(1)}, bf16[1536,512]{1,0:T(8,128)(2,1)S(1)}) custom-call(bf16[256,1536]{1,0:T(8,128)(2,1)S(1)} %all_gather.6.s_ref, bf16[32,128,128]{2,1,0:T(8,128)(2,1)S(1)} %all-to-all-done.mine_ref, bf16[32,128,128]{2,1,0:T(8,128)(2,1)S(1)} %collective-permute-done.other_ref), custom_call_target="tpu_custom_call" | custom-call | flops 402653184 | bytes 4194304 | tf_op jit(solution)/shard_map/pallas_call | solution.py:193
  56.1 14.2 %all_to_all.15.parts_ref = s16[4,272,128]{2,1,0:T(8,128)(2,1)S(1)} all-to-all(s16[4,272,128]{2,1,0:T(8,128)(2,1)S(1)} %get-tuple-element.16), channel_id=1, replica_groups={{3,0,1,2},{7,4,5,6},{11,8,9,10},{15,12,13,14},{19,16,17,18},{23,20,21,2..., dimensions={0} | all-to-all | bytes 557056 | tf_op jit(solution)/shard_map/all_to_all | solution.py:194
  70.3 0.0 copy-done.1
  70.3 0.1 shard_map.43.square_ref
  70.4 25.3 %all_gather.7.s_ref = bf16[256,1536]{1,0:T(8,128)(2,1)S(1)} all-gather(bf16[256,128]{1,0:T(8,128)(2,1)S(1)} %shard_map.43.square_ref), channel_id=1, replica_groups=mesh['yl'=2,'x'=4,'core'=2,'z'=12,'yh'=4] {'z'}, dimensions={1}, use_global_device_ids=true | all-gather | bytes 851968 | tf_op jit(solution)/shard_map/all_gather | solution.py:196
  95.7 1.1 %shard_map.44 = (s16[4,272,128]{2,1,0:T(8,128)(2,1)S(1)}, bf16[256,128]{1,0:T(8,128)(2,1)}) custom-call(bf16[256,1536]{1,0:T(8,128)(2,1)S(1)} %all_gather.7.s_ref, bf16[1536,512]{1,0:T(8,128)(2,1)S(1)} %get-tuple-element.17.mk_ref, bf16[256,128]{1,0:T(8,128)(2,1)S(1)} %shard_map.43.square_ref), custom_call_target="tpu_custom_call" | custom-call | flops 402653184 | bytes 4194304 | tf_op jit(solution)/shard_map/pallas_call | solution.py:197
  96.8 12.3 %all_to_all.16.parts_ref = s16[4,272,128]{2,1,0:T(8,128)(2,1)S(1)} all-to-all(s16[4,272,128]{2,1,0:T(8,128)(2,1)S(1)} %get-tuple-element.19), channel_id=1, replica_groups={{2,3,0,1},{6,7,4,5},{10,11,8,9},{14,15,12,13},{18,19,16,17},{22,23,20,2..., dimensions={0} | all-to-all | bytes 557056 | tf_op jit(solution)/shard_map/all_to_all | solution.py:206
  109.1 0.8 shard_map.45
Async XLA Ops:
  2.6 16.8 %copy-start = (bf16[256,128]{1,0:T(8,128)(2,1)S(1)}, bf16[256,128]{1,0:T(8,128)(2,1)}, u32[]{:S(2)}) copy-start(bf16[256,128]{1,0:T(8,128)(2,1)} %get-tuple-element.13.slab_ref) | copy-start | bytes 196612
  2.7 47.2 %all-to-all-start = ((bf16[32,128,128]{2,1,0:T(8,128)(2,1)}), bf16[32,128,128]{2,1,0:T(8,128)(2,1)S(1)}, u32[]{:S(2)}, u32[]{:S(2)}) async-start(bf16[32,128,128]{2,1,0:T(8,128)(2,1)} %get-tuple-element.12), calls=%async_computation | async-start | bytes 2097152 | tf_op jit(solution)/shard_map/all_to_all | solution.py:186
  49.8 20.4 %copy-start.1 = (f32[16,128]{1,0:T(8,128)S(1)}, f32[16,128]{1,0:T(8,128)}, u32[]{:S(2)}) copy-start(f32[16,128]{1,0:T(8,128)} %get-tuple-element.11.mask_ref) | copy-start | bytes 24580
  49.8 4.7 %collective-permute-start = (bf16[32,128,128]{2,1,0:T(8,128)(2,1)S(1)}, bf16[32,128,128]{2,1,0:T(8,128)(2,1)S(1)}, u32[]{:S(2)}, u32[]{:S(2)}) collective-permute-start(bf16[32,128,128]{2,1,0:T(8,128)(2,1)S(1)} %all-to-all-done.mine_ref), channel_id=1, source_target_pairs={{0,48},{48,0},{1,49},{49,1},{2,50},{50,2},{3,51},{51,3},{4,52},{52... | collective-permute-start | bytes 3145736 | tf_op jit(solution)/shard_map/ppermute | solution.py:189

commit v10 on v9

--- a/solution.py
+++ b/solution.py
@@ -17,7 +17,7 @@
 PLACES = [2, 3, 0, 1]
 FIRST_PLACES = [3, 0, 1, 2]
 SECOND_PLACES = [2, 3, 0, 1]
-X_PLACES = [2, 3, 0, 1]
+X_PLACES = [1, 2, 3, 0]
 YL_PLACES = [0, 1]
 LIMIT = 24 * 1024 * 1024
 

time: 112 us -> 112 us (level)
  no operation moved by 1% of the time
where the time goes in v10:
time: 112 us; the launch traced here: 110 us
  blocking collectives  81.5 us (73%)
  starting transfers between devices  19.4 us (17%)
  Pallas kernels  5.61 us (5%)
  waiting for transfers between devices  2.63 us (2%)
    all_gather x1, blocking collectives, local(): gathered = lax.all_gather(slab, 'z', axis=1, tiled=True)  30.7 us
    all_gather x1, blocking collectives, local(): gathered = lax.all_gather(square, 'z', axis=1, tiled=True)  24.4 us
    all_to_all x1, starting transfers between devices, local(): lax.all_to_all(send, ('yl', 'x', 'yh'), 0, 0, tiled=True, axis_index_grou...  17.3 us
    all_to_all x1, blocking collectives, local(): lax.all_to_all(parts, 'yh', 0, 0, tiled=True, axis_index_groups=[FIRST_PL...  14.2 us
    all_to_all x1, blocking collectives, local(): lax.all_to_all(parts, 'yh', 0, 0, tiled=True, axis_index_groups=[SECOND_P...  12.3 us
    ppermute x1, waiting for transfers between devices, local(): other = lax.ppermute(mine, 'core', [(0, 1), (1, 0)])  2.63 us
  transfers between devices with their start and end apart: 2, of which 1 were waited for; matrix products, arithmetic and copies ran while one was open for 0% of the time, Pallas kernels for 0%

profile of v10, /device:TPU:6, one launch (start us, length us, event | category | flops | bytes accessed | tf_op | source)
XLA Modules:
  0.0 109.8 jit_solution(3488790172023770303)
XLA Ops:
  0.6 2.0 %shard_map.41 = (bf16[256,128]{1,0:T(8,128)(2,1)}, f32[16,128]{1,0:T(8,128)}, bf16[32,128,128]{2,1,0:T(8,128)(2,1)}) custom-call(s32[3]{0:T(128)} %bitcast.1, bf16[384,128]{1,0:T(8,128)(2,1)} %values_hbm.1), custom_call_target="tpu_custom_call" | custom-call | tf_op jit(solution)/shard_map/pallas_call | solution.py:169
  2.6 0.0 copy-start
  2.7 17.3 %all-to-all-start = ((bf16[32,128,128]{2,1,0:T(8,128)(2,1)}), bf16[32,128,128]{2,1,0:T(8,128)(2,1)S(1)}, u32[]{:S(2)}, u32[]{:S(2)}) async-start(bf16[32,128,128]{2,1,0:T(8,128)(2,1)} %get-tuple-element.12), calls=%async_computation | async-start | bytes 2097152 | tf_op jit(solution)/shard_map/all_to_all | solution.py:186
  20.0 0.0 copy-done
  20.0 30.7 %all_gather.6.s_ref = bf16[256,1536]{1,0:T(8,128)(2,1)S(1)} all-gather(bf16[256,128]{1,0:T(8,128)(2,1)S(1)} %copy-done), channel_id=1, replica_groups=mesh['yl'=2,'x'=4,'core'=2,'z'=12,'yh'=4] {'z'}, dimensions={1}, use_global_device_ids=true | all-gather | bytes 851968 | tf_op jit(solution)/shard_map/all_gather | solution.py:187
  50.7 0.0 copy-start.1
  50.7 0.0 all-to-all-done.mine_ref
  50.7 2.0 %collective-permute-start = (bf16[32,128,128]{2,1,0:T(8,128)(2,1)S(1)}, bf16[32,128,128]{2,1,0:T(8,128)(2,1)S(1)}, u32[]{:S(2)}, u32[]{:S(2)}) collective-permute-start(bf16[32,128,128]{2,1,0:T(8,128)(2,1)S(1)} %all-to-all-done.mine_ref), channel_id=1, source_target_pairs={{0,48},{48,0},{1,49},{49,1},{2,50},{50,2},{3,51},{51,3},{4,52},{52... | collective-permute-start | bytes 3145736 | tf_op jit(solution)/shard_map/ppermute | solution.py:189
  52.8 2.6 %collective-permute-done.other_ref = bf16[32,128,128]{2,1,0:T(8,128)(2,1)S(1)} collective-permute-done((bf16[32,128,128]{2,1,0:T(8,128)(2,1)S(1)}, bf16[32,128,128]{2,1,0:T(8,128)(2,1)S(1)}, u32[]{:S(2)}, u32[]{:S(2)}) %collective-permute-start) | collective-permute-done | bytes 1048608 | tf_op jit(solution)/shard_map/ppermute | solution.py:189
  55.4 1.6 %shard_map.42 = (s16[4,272,128]{2,1,0:T(8,128)(2,1)S(1)}, bf16[1536,512]{1,0:T(8,128)(2,1)S(1)}) custom-call(bf16[256,1536]{1,0:T(8,128)(2,1)S(1)} %all_gather.6.s_ref, bf16[32,128,128]{2,1,0:T(8,128)(2,1)S(1)} %all-to-all-done.mine_ref, bf16[32,128,128]{2,1,0:T(8,128)(2,1)S(1)} %collective-permute-done.other_ref), custom_call_target="tpu_custom_call" | custom-call | flops 402653184 | bytes 4194304 | tf_op jit(solution)/shard_map/pallas_call | solution.py:193
  57.0 14.2 %all_to_all.15.parts_ref = s16[4,272,128]{2,1,0:T(8,128)(2,1)S(1)} all-to-all(s16[4,272,128]{2,1,0:T(8,128)(2,1)S(1)} %get-tuple-element.16), channel_id=1, replica_groups={{3,0,1,2},{7,4,5,6},{11,8,9,10},{15,12,13,14},{19,16,17,18},{23,20,21,2..., dimensions={0} | all-to-all | bytes 557056 | tf_op jit(solution)/shard_map/all_to_all | solution.py:194
  71.1 0.0 copy-done.1
  71.1 0.1 shard_map.43.square_ref
  71.3 24.4 %all_gather.7.s_ref = bf16[256,1536]{1,0:T(8,128)(2,1)S(1)} all-gather(bf16[256,128]{1,0:T(8,128)(2,1)S(1)} %shard_map.43.square_ref), channel_id=1, replica_groups=mesh['yl'=2,'x'=4,'core'=2,'z'=12,'yh'=4] {'z'}, dimensions={1}, use_global_device_ids=true | all-gather | bytes 851968 | tf_op jit(solution)/shard_map/all_gather | solution.py:196
  95.6 1.1 %shard_map.44 = (s16[4,272,128]{2,1,0:T(8,128)(2,1)S(1)}, bf16[256,128]{1,0:T(8,128)(2,1)}) custom-call(bf16[256,1536]{1,0:T(8,128)(2,1)S(1)} %all_gather.7.s_ref, bf16[1536,512]{1,0:T(8,128)(2,1)S(1)} %get-tuple-element.17.mk_ref, bf16[256,128]{1,0:T(8,128)(2,1)S(1)} %shard_map.43.square_ref), custom_call_target="tpu_custom_call" | custom-call | flops 402653184 | bytes 4194304 | tf_op jit(solution)/shard_map/pallas_call | solution.py:197
  96.8 12.3 %all_to_all.16.parts_ref = s16[4,272,128]{2,1,0:T(8,128)(2,1)S(1)} all-to-all(s16[4,272,128]{2,1,0:T(8,128)(2,1)S(1)} %get-tuple-element.19), channel_id=1, replica_groups={{2,3,0,1},{6,7,4,5},{10,11,8,9},{14,15,12,13},{18,19,16,17},{22,23,20,2..., dimensions={0} | all-to-all | bytes 557056 | tf_op jit(solution)/shard_map/all_to_all | solution.py:206
  109.1 0.8 shard_map.45
Async XLA Ops:
  2.6 17.4 %copy-start = (bf16[256,128]{1,0:T(8,128)(2,1)S(1)}, bf16[256,128]{1,0:T(8,128)(2,1)}, u32[]{:S(2)}) copy-start(bf16[256,128]{1,0:T(8,128)(2,1)} %get-tuple-element.13.slab_ref) | copy-start | bytes 196612
  2.7 48.1 %all-to-all-start = ((bf16[32,128,128]{2,1,0:T(8,128)(2,1)}), bf16[32,128,128]{2,1,0:T(8,128)(2,1)S(1)}, u32[]{:S(2)}, u32[]{:S(2)}) async-start(bf16[32,128,128]{2,1,0:T(8,128)(2,1)} %get-tuple-element.12), calls=%async_computation | async-start | bytes 2097152 | tf_op jit(solution)/shard_map/all_to_all | solution.py:186
  50.7 20.4 %copy-start.1 = (f32[16,128]{1,0:T(8,128)S(1)}, f32[16,128]{1,0:T(8,128)}, u32[]{:S(2)}) copy-start(f32[16,128]{1,0:T(8,128)} %get-tuple-element.11.mask_ref) | copy-start | bytes 24580
  50.7 4.7 %collective-permute-start = (bf16[32,128,128]{2,1,0:T(8,128)(2,1)S(1)}, bf16[32,128,128]{2,1,0:T(8,128)(2,1)S(1)}, u32[]{:S(2)}, u32[]{:S(2)}) collective-permute-start(bf16[32,128,128]{2,1,0:T(8,128)(2,1)S(1)} %all-to-all-done.mine_ref), channel_id=1, source_target_pairs={{0,48},{48,0},{1,49},{49,1},{2,50},{50,2},{3,51},{51,3},{4,52},{52... | collective-permute-start | bytes 3145736 | tf_op jit(solution)/shard_map/ppermute | solution.py:189

commit v11 on v9

--- a/solution.py
+++ b/solution.py
@@ -18,7 +18,7 @@
 FIRST_PLACES = [3, 0, 1, 2]
 SECOND_PLACES = [2, 3, 0, 1]
 X_PLACES = [2, 3, 0, 1]
-YL_PLACES = [0, 1]
+YL_PLACES = [1, 0]
 LIMIT = 24 * 1024 * 1024
 
 

time: 112 us -> 111 us (level)
  no operation moved by 1% of the time
where the time goes in v11:
time: 111 us; the launch traced here: 109 us
  blocking collectives  82.5 us (74%)
  starting transfers between devices  17.9 us (16%)
  Pallas kernels  5.62 us (5%)
  waiting for transfers between devices  2.63 us (2%)
    all_gather x1, blocking collectives, local(): gathered = lax.all_gather(slab, 'z', axis=1, tiled=True)  30.6 us
    all_gather x1, blocking collectives, local(): gathered = lax.all_gather(square, 'z', axis=1, tiled=True)  24.6 us
    all_to_all x1, starting transfers between devices, local(): lax.all_to_all(send, ('yl', 'x', 'yh'), 0, 0, tiled=True, axis_index_grou...  15.9 us
    all_to_all x1, blocking collectives, local(): lax.all_to_all(parts, 'yh', 0, 0, tiled=True, axis_index_groups=[FIRST_PL...  15 us
    all_to_all x1, blocking collectives, local(): lax.all_to_all(parts, 'yh', 0, 0, tiled=True, axis_index_groups=[SECOND_P...  12.3 us
    ppermute x1, waiting for transfers between devices, local(): other = lax.ppermute(mine, 'core', [(0, 1), (1, 0)])  2.63 us
  transfers between devices with their start and end apart: 2, of which 1 were waited for; matrix products, arithmetic and copies ran while one was open for 0% of the time, Pallas kernels for 0%

profile of v11, /device:TPU:6, one launch (start us, length us, event | category | flops | bytes accessed | tf_op | source)
XLA Modules:
  0.0 109.3 jit_solution(12291178999297343148)
XLA Ops:
  0.6 2.0 %shard_map.41 = (bf16[256,128]{1,0:T(8,128)(2,1)}, f32[16,128]{1,0:T(8,128)}, bf16[32,128,128]{2,1,0:T(8,128)(2,1)}) custom-call(s32[3]{0:T(128)} %bitcast.1, bf16[384,128]{1,0:T(8,128)(2,1)} %values_hbm.1), custom_call_target="tpu_custom_call" | custom-call | tf_op jit(solution)/shard_map/pallas_call | solution.py:169
  2.6 0.0 copy-start
  2.7 15.9 %all-to-all-start = ((bf16[32,128,128]{2,1,0:T(8,128)(2,1)}), bf16[32,128,128]{2,1,0:T(8,128)(2,1)S(1)}, u32[]{:S(2)}, u32[]{:S(2)}) async-start(bf16[32,128,128]{2,1,0:T(8,128)(2,1)} %get-tuple-element.12), calls=%async_computation | async-start | bytes 2097152 | tf_op jit(solution)/shard_map/all_to_all | solution.py:186
  18.5 0.0 copy-done
  18.5 30.6 %all_gather.6.s_ref = bf16[256,1536]{1,0:T(8,128)(2,1)S(1)} all-gather(bf16[256,128]{1,0:T(8,128)(2,1)S(1)} %copy-done), channel_id=1, replica_groups=mesh['yl'=2,'x'=4,'core'=2,'z'=12,'yh'=4] {'z'}, dimensions={1}, use_global_device_ids=true | all-gather | bytes 851968 | tf_op jit(solution)/shard_map/all_gather | solution.py:187
  49.1 0.0 copy-start.1
  49.2 0.0 all-to-all-done.mine_ref
  49.2 2.0 %collective-permute-start = (bf16[32,128,128]{2,1,0:T(8,128)(2,1)S(1)}, bf16[32,128,128]{2,1,0:T(8,128)(2,1)S(1)}, u32[]{:S(2)}, u32[]{:S(2)}) collective-permute-start(bf16[32,128,128]{2,1,0:T(8,128)(2,1)S(1)} %all-to-all-done.mine_ref), channel_id=1, source_target_pairs={{0,48},{48,0},{1,49},{49,1},{2,50},{50,2},{3,51},{51,3},{4,52},{52... | collective-permute-start | bytes 3145736 | tf_op jit(solution)/shard_map/ppermute | solution.py:189
  51.2 2.6 %collective-permute-done.other_ref = bf16[32,128,128]{2,1,0:T(8,128)(2,1)S(1)} collective-permute-done((bf16[32,128,128]{2,1,0:T(8,128)(2,1)S(1)}, bf16[32,128,128]{2,1,0:T(8,128)(2,1)S(1)}, u32[]{:S(2)}, u32[]{:S(2)}) %collective-permute-start) | collective-permute-done | bytes 1048608 | tf_op jit(solution)/shard_map/ppermute | solution.py:189
  53.8 1.6 %shard_map.42 = (s16[4,272,128]{2,1,0:T(8,128)(2,1)S(1)}, bf16[1536,512]{1,0:T(8,128)(2,1)S(1)}) custom-call(bf16[256,1536]{1,0:T(8,128)(2,1)S(1)} %all_gather.6.s_ref, bf16[32,128,128]{2,1,0:T(8,128)(2,1)S(1)} %all-to-all-done.mine_ref, bf16[32,128,128]{2,1,0:T(8,128)(2,1)S(1)} %collective-permute-done.other_ref), custom_call_target="tpu_custom_call" | custom-call | flops 402653184 | bytes 4194304 | tf_op jit(solution)/shard_map/pallas_call | solution.py:193
  55.4 15.0 %all_to_all.15.parts_ref = s16[4,272,128]{2,1,0:T(8,128)(2,1)S(1)} all-to-all(s16[4,272,128]{2,1,0:T(8,128)(2,1)S(1)} %get-tuple-element.16), channel_id=1, replica_groups={{3,0,1,2},{7,4,5,6},{11,8,9,10},{15,12,13,14},{19,16,17,18},{23,20,21,2..., dimensions={0} | all-to-all | bytes 557056 | tf_op jit(solution)/shard_map/all_to_all | solution.py:194
  70.4 0.0 copy-done.1
  70.4 0.1 shard_map.43.square_ref
  70.5 24.6 %all_gather.7.s_ref = bf16[256,1536]{1,0:T(8,128)(2,1)S(1)} all-gather(bf16[256,128]{1,0:T(8,128)(2,1)S(1)} %shard_map.43.square_ref), channel_id=1, replica_groups=mesh['yl'=2,'x'=4,'core'=2,'z'=12,'yh'=4] {'z'}, dimensions={1}, use_global_device_ids=true | all-gather | bytes 851968 | tf_op jit(solution)/shard_map/all_gather | solution.py:196
  95.1 1.1 %shard_map.44 = (s16[4,272,128]{2,1,0:T(8,128)(2,1)S(1)}, bf16[256,128]{1,0:T(8,128)(2,1)}) custom-call(bf16[256,1536]{1,0:T(8,128)(2,1)S(1)} %all_gather.7.s_ref, bf16[1536,512]{1,0:T(8,128)(2,1)S(1)} %get-tuple-element.17.mk_ref, bf16[256,128]{1,0:T(8,128)(2,1)S(1)} %shard_map.43.square_ref), custom_call_target="tpu_custom_call" | custom-call | flops 402653184 | bytes 4194304 | tf_op jit(solution)/shard_map/pallas_call | solution.py:197
  96.2 12.3 %all_to_all.16.parts_ref = s16[4,272,128]{2,1,0:T(8,128)(2,1)S(1)} all-to-all(s16[4,272,128]{2,1,0:T(8,128)(2,1)S(1)} %get-tuple-element.19), channel_id=1, replica_groups={{2,3,0,1},{6,7,4,5},{10,11,8,9},{14,15,12,13},{18,19,16,17},{22,23,20,2..., dimensions={0} | all-to-all | bytes 557056 | tf_op jit(solution)/shard_map/all_to_all | solution.py:206
  108.5 0.8 shard_map.45
Async XLA Ops:
  2.6 15.9 %copy-start = (bf16[256,128]{1,0:T(8,128)(2,1)S(1)}, bf16[256,128]{1,0:T(8,128)(2,1)}, u32[]{:S(2)}) copy-start(bf16[256,128]{1,0:T(8,128)(2,1)} %get-tuple-element.13.slab_ref) | copy-start | bytes 196612
  2.7 46.5 %all-to-all-start = ((bf16[32,128,128]{2,1,0:T(8,128)(2,1)}), bf16[32,128,128]{2,1,0:T(8,128)(2,1)S(1)}, u32[]{:S(2)}, u32[]{:S(2)}) async-start(bf16[32,128,128]{2,1,0:T(8,128)(2,1)} %get-tuple-element.12), calls=%async_computation | async-start | bytes 2097152 | tf_op jit(solution)/shard_map/all_to_all | solution.py:186
  49.1 21.2 %copy-start.1 = (f32[16,128]{1,0:T(8,128)S(1)}, f32[16,128]{1,0:T(8,128)}, u32[]{:S(2)}) copy-start(f32[16,128]{1,0:T(8,128)} %get-tuple-element.11.mask_ref) | copy-start | bytes 24580
  49.2 4.7 %collective-permute-start = (bf16[32,128,128]{2,1,0:T(8,128)(2,1)S(1)}, bf16[32,128,128]{2,1,0:T(8,128)(2,1)S(1)}, u32[]{:S(2)}, u32[]{:S(2)}) collective-permute-start(bf16[32,128,128]{2,1,0:T(8,128)(2,1)S(1)} %all-to-all-done.mine_ref), channel_id=1, source_target_pairs={{0,48},{48,0},{1,49},{49,1},{2,50},{50,2},{3,51},{51,3},{4,52},{52... | collective-permute-start | bytes 3145736 | tf_op jit(solution)/shard_map/ppermute | solution.py:189
